TPU v7x, 32 devices: a whole 2x2x4 slice. The times are simulated.
32 devices in a mesh: batch: 16 (over z, y, x), blk: 2 (over core).
Axes of the slice: x: 2, y: 2, z: 4, core: 2. Of those that a mesh axis runs over, the one named last changes fastest.
Arguments:
- hidden: bfloat16 [32, 512, 1024], P('batch', 'blk'), may hold values from -6 to 6
- cotangent: bfloat16 [32, 512, 1024], P('batch', 'blk'), may hold values from -6 to 6
- lengths: int32 [32], P('batch'), may hold values from 257 to 512, as said below
- separators: int32 [32], P('batch'), may hold values from 1 to 510, as said below
- type_table: bfloat16 [2, 1024], replicated, may hold values from -3 to 3
- projection_weight: bfloat16 [2, 1024, 3072], P(None, 'batch'), may hold values from -0.1875 to 0.1875
- output_weight: bfloat16 [2, 1024, 1024], P(None, 'batch'), may hold values from -1.5 to 1.5
- inner_weight: bfloat16 [2, 1024, 4096], P(None, 'batch'), may hold values from -0.1875 to 0.1875
- outer_weight: bfloat16 [2, 4096, 1024], P(None, 'batch'), may hold values from -0.09375 to 0.09375
- query_bias: float32 [2, 1024], replicated, may hold values from -3 to 3
- value_bias: float32 [2, 1024], replicated, may hold values from -3 to 3
- output_bias: float32 [2, 1024], replicated, may hold values from -2 to 2
- inner_bias: float32 [2, 4096], replicated, may hold values from -3 to 3
- outer_bias: float32 [2, 1024], replicated, may hold values from -2 to 2
- first_gain: float32 [2, 1024], replicated, may hold values from 0.5 to 1.5
- first_shift: float32 [2, 1024], replicated, may hold values from -2 to 2
- second_gain: float32 [2, 1024], replicated, may hold values from 0.5 to 1.5
- second_shift: float32 [2, 1024], replicated, may hold values from -2 to 2
Outputs:
- layer_output: bfloat16 [32, 512, 1024], P('batch', 'blk')
- input_gradient: bfloat16 [32, 512, 1024], P('batch', 'blk')
- query_bias_gradient: float32 [2, 1024], replicated
- value_bias_gradient: float32 [2, 1024], replicated
- output_bias_gradient: float32 [2, 1024], replicated
- inner_bias_gradient: float32 [2, 4096], replicated
- outer_bias_gradient: float32 [2, 1024], replicated
- first_shift_gradient: float32 [2, 1024], replicated
- second_shift_gradient: float32 [2, 1024], replicated
Inputs may be any that keep to these rules, and one draw needn't show every extreme that they name: `lengths`: every pair's length exceeds 256; in every draw some pair is 512 long. separators[s] <= lengths[s] - 2; in every draw some pair has its separator at 1 and some pair at 510.
All inputs are finite; a program needn't handle non-finite values.
Results may differ from a plain program's by a relative error of at most 0.019.
Values may be sent and summed in bfloat16 or wider, within the bound.
A program may use at most 192 MiB of HBM per device.

v0:
```python
import jax
import jax.numpy as jnp
from jax import lax
from jax.sharding import PartitionSpec as P

D = 1024
HEADS = 16
HEAD = 64
LAYERS = 2


EPSILON = 1e-12
MASKED = -1000000000.0


def layer_norm(summed, norm_gain, norm_shift):
    average = jnp.mean(summed, axis=-1, keepdims=True)
    centred = summed - average
    variance = jnp.mean(centred * centred, axis=-1, keepdims=True)
    return centred * lax.rsqrt(variance + EPSILON) * norm_gain + norm_shift


def gelu_exact(values):
    return jax.nn.gelu(values, approximate=False)


def project(left, weight):
    return jnp.einsum("gtd,de->gte", left, weight, preferred_element_type=jnp.float32)


def project_back(grad_rows, weight):
    return jnp.einsum("gte,de->gtd", grad_rows, weight, preferred_element_type=jnp.float32)


def token_sum(values):
    return jnp.sum(values, axis=(0, 1))


def split_heads(values, row_count):
    group_count = values.shape[0]
    return jnp.moveaxis(values.reshape(group_count, row_count, 2, HEADS // 2, HEAD), 2, 0)


def join_heads(values):
    reordered = jnp.moveaxis(values, 0, 2)
    return reordered.reshape(reordered.shape[0], reordered.shape[1], -1)


def block_scores(query_block, key_block, key_mask, score_scale):
    product = jnp.einsum(
        "gqhe,gkhe->ghqk", query_block, key_block, preferred_element_type=jnp.float32
    )
    return jnp.where(key_mask, product * score_scale, MASKED)


def attend_block(block_inputs, key_mask, score_scale):
    query_block, key_block, value_block = block_inputs
    scores = block_scores(query_block, key_block, key_mask, score_scale)
    largest = jnp.max(scores, axis=-1, keepdims=True)
    exponent = jnp.exp(scores - largest)
    denominator = jnp.sum(exponent, axis=-1, keepdims=True)
    weights_soft = (exponent / denominator).astype(jnp.bfloat16)
    context = jnp.einsum(
        "ghqk,gkhe->gqhe", weights_soft, value_block, preferred_element_type=jnp.float32
    )
    return (context.astype(jnp.bfloat16), largest, denominator)


def attend_back(block_inputs, key_mask, score_scale):
    query_block, key_block, value_block, largest, denominator, grad_block = block_inputs
    scores = block_scores(query_block, key_block, key_mask, score_scale)
    probability = jnp.exp(scores - largest) / denominator
    grad_prob = jnp.einsum(
        "gqhe,gkhe->ghqk", grad_block, value_block, preferred_element_type=jnp.float32
    )
    row_dot = jnp.sum(grad_prob * probability, axis=-1, keepdims=True)
    grad_scores = (probability * (grad_prob - row_dot) * score_scale).astype(jnp.bfloat16)
    grad_query = jnp.einsum(
        "ghqk,gkhe->gqhe", grad_scores, key_block, preferred_element_type=jnp.float32
    )
    grad_key = jnp.einsum(
        "ghqk,gqhe->gkhe", grad_scores, query_block, preferred_element_type=jnp.float32
    )
    grad_value = jnp.einsum(
        "ghqk,gqhe->gkhe",
        probability.astype(jnp.bfloat16),
        grad_block,
        preferred_element_type=jnp.float32,
    )
    return (grad_query, grad_key, grad_value)


def on_device(
    hidden,
    cotangent,
    lengths,
    separators,
    type_table,
    projection_weight,
    output_weight,
    inner_weight,
    outer_weight,
    query_bias,
    value_bias,
    output_bias,
    inner_bias,
    outer_bias,
    first_gain,
    first_shift,
    second_gain,
    second_shift,
):
    groups, span_rows, _unused = hidden.shape
    full_length = span_rows * lax.axis_size("blk")
    score_scale = HEAD ** (-0.5)
    position = lax.axis_index("blk") * span_rows + jnp.arange(span_rows)
    second_part = (position[None, :] > separators[:, None]).astype(jnp.float32)
    type_rows = type_table.astype(jnp.float32)
    current = (
        hidden.astype(jnp.float32)
        + type_rows[0]
        + second_part[:, :, None] * (type_rows[1] - type_rows[0])
    )
    key_valid = jnp.arange(full_length)[None, :] < lengths[:, None]
    key_mask = key_valid[:, None, None, :]

    def forward_block(block_inputs):
        return attend_block(block_inputs, key_mask, score_scale)

    def backward_block(block_inputs):
        return attend_back(block_inputs, key_mask, score_scale)

    stored = []
    kept_weights = []
    for layer_index in range(LAYERS):
        gathered = (
            lax.all_gather(projection_weight[layer_index], "batch", axis=0, tiled=True),
            lax.all_gather(output_weight[layer_index], "batch", axis=0, tiled=True),
            lax.all_gather(inner_weight[layer_index], "batch", axis=0, tiled=True),
            lax.all_gather(outer_weight[layer_index], "batch", axis=0, tiled=True),
        )
        kept_weights.append(gathered)
        w_triple, w_output, w_inner, w_outer = gathered
        projected = project(current.astype(jnp.bfloat16), w_triple)
        queries = (projected[..., :D] + query_bias[layer_index]).astype(jnp.bfloat16)
        keys_own = projected[..., D : 2 * D].astype(jnp.bfloat16)
        values_own = (projected[..., 2 * D :] + value_bias[layer_index]).astype(jnp.bfloat16)
        keys_all, values_all = (
            lax.all_gather(keys_own, "blk", axis=1, tiled=True),
            lax.all_gather(values_own, "blk", axis=1, tiled=True),
        )
        query_split = split_heads(queries, span_rows)
        key_split = split_heads(keys_all, full_length)
        value_split = split_heads(values_all, full_length)
        context_split, largest, denominator = lax.map(
            forward_block, (query_split, key_split, value_split)
        )
        context = join_heads(context_split)
        first_in = current + project(context, w_output) + output_bias[layer_index]
        middle = layer_norm(first_in, first_gain[layer_index], first_shift[layer_index])
        hidden_pre = project(middle.astype(jnp.bfloat16), w_inner) + inner_bias[layer_index]
        activated = gelu_exact(hidden_pre).astype(jnp.bfloat16)
        second_in = middle + project(activated, w_outer) + outer_bias[layer_index]
        stored.append(
            (
                query_split,
                key_split,
                value_split,
                largest,
                denominator,
                first_in,
                middle,
                hidden_pre,
                second_in,
            )
        )
        current = layer_norm(second_in, second_gain[layer_index], second_shift[layer_index])
    layer_output = current.astype(jnp.bfloat16)
    grad_rows = cotangent.astype(jnp.float32)
    collected = []
    for layer_index in reversed(range(LAYERS)):
        (
            query_split,
            key_split,
            value_split,
            largest,
            denominator,
            first_in,
            middle,
            hidden_pre,
            second_in,
        ) = stored[layer_index]
        gathered = (
            lax.all_gather(projection_weight[layer_index], "batch", axis=0, tiled=True),
            lax.all_gather(output_weight[layer_index], "batch", axis=0, tiled=True),
            lax.all_gather(inner_weight[layer_index], "batch", axis=0, tiled=True),
            lax.all_gather(outer_weight[layer_index], "batch", axis=0, tiled=True),
        )
        w_triple, w_output, w_inner, w_outer = gathered
        second_value, second_back = jax.vjp(
            lambda summed, norm_shift: layer_norm(summed, second_gain[layer_index], norm_shift),
            second_in,
            second_shift[layer_index],
        )
        grad_second, grad_second_shift = second_back(grad_rows)
        grad_outer_bias = token_sum(grad_second)
        grad_activated = project_back(grad_second.astype(jnp.bfloat16), w_outer)
        gelu_value, gelu_back = jax.vjp(gelu_exact, hidden_pre)
        grad_hidden = gelu_back(grad_activated)[0]
        grad_inner_bias = token_sum(grad_hidden)
        grad_middle = grad_second + project_back(grad_hidden.astype(jnp.bfloat16), w_inner)
        first_value, first_back = jax.vjp(
            lambda summed, norm_shift: layer_norm(summed, first_gain[layer_index], norm_shift),
            first_in,
            first_shift[layer_index],
        )
        grad_first, grad_first_shift = first_back(grad_middle)
        grad_output_bias = token_sum(grad_first)
        grad_context = project_back(grad_first.astype(jnp.bfloat16), w_output).astype(jnp.bfloat16)
        grad_split = split_heads(grad_context, span_rows)
        query_grads, key_grads, value_grads = lax.map(
            backward_block, (query_split, key_split, value_split, largest, denominator, grad_split)
        )
        grad_queries = join_heads(query_grads)
        grad_keys_own, grad_values_own = (
            lax.psum_scatter(
                join_heads(key_grads).astype(jnp.bfloat16), "blk", scatter_dimension=1, tiled=True
            ).astype(jnp.float32),
            lax.psum_scatter(
                join_heads(value_grads).astype(jnp.bfloat16), "blk", scatter_dimension=1, tiled=True
            ).astype(jnp.float32),
        )
        grad_query_bias = token_sum(grad_queries)
        grad_value_bias = token_sum(grad_values_own)
        grad_mixed = jnp.concatenate(
            (
                grad_queries.astype(jnp.bfloat16),
                grad_keys_own.astype(jnp.bfloat16),
                grad_values_own.astype(jnp.bfloat16),
            ),
            axis=2,
        )
        grad_rows = grad_first + project_back(grad_mixed, w_triple)
        local_terms = (
            grad_query_bias,
            grad_value_bias,
            grad_output_bias,
            grad_inner_bias,
            grad_outer_bias,
            grad_first_shift,
            grad_second_shift,
        )
        local_terms = lax.psum(
            (
                local_terms[0],
                local_terms[1],
                local_terms[2],
                local_terms[3],
                local_terms[4],
                local_terms[5],
                local_terms[6],
            ),
            ("batch", "blk"),
        )
        collected.insert(0, local_terms)
    stacked = tuple(
        (jnp.stack([terms_layer[member] for terms_layer in collected]) for member in range(7))
    )
    return (
        layer_output,
        grad_rows.astype(jnp.bfloat16),
        stacked[0],
        stacked[1],
        stacked[2],
        stacked[3],
        stacked[4],
        stacked[5],
        stacked[6],
    )


def solution(mesh):
    return jax.shard_map(
        on_device,
        mesh=mesh,
        in_specs=(
            P("batch", "blk", None),
            P("batch", "blk", None),
            P("batch"),
            P("batch"),
            P(),
            P(None, "batch", None),
            P(None, "batch", None),
            P(None, "batch", None),
            P(None, "batch", None),
            P(),
            P(),
            P(),
            P(),
            P(),
            P(),
            P(),
            P(),
            P(),
        ),
        out_specs=(
            P("batch", "blk", None),
            P("batch", "blk", None),
            P(),
            P(),
            P(),
            P(),
            P(),
            P(),
            P(),
        ),
        check_vma=False,
    )
```

profile of v0, /device:TPU:0, one launch (start us, length us, event | category | flops | bytes accessed | tf_op | source)
XLA Modules:
  0.0 1332.0 jit_solution(8209811074539940321)
XLA Ops:
  12.4 95.8 %all-gather.29.cloned.1.call-done = bf16[1,1024,3072]{2,1,0:T(8,128)(2,1)} async-done(((bf16[1,64,3072]{2,1,0:T(8,128)(2,1)}), bf16[1,1024,3072]{2,1,0:T(8,128)(2,1)}) %all-gather.29.cloned.1.call-update) | async-done | bytes 6291472 | tf_op jit(solution)/shard_map/all_gather | solution.py:137
  108.2 5.9 fusion.172
  136.0 5.4 all-gather.23.cloned.1.call-done
  149.6 17.0 %while.60 = (s32[]{:T(128)}, bf16[2,2,256,8,64]{2,4,3,0,1:T(8,128)(2,1)}, f32[2,2,8,256,1]{3,2,1,4,0:T(8,128)S(1)}, f32[2,2,8,256,1]{3,2,1,4,0:T(8,128)S(1)}, bf...) while((s32[]{:T(128)}, ...), condition=%wide.region_3.4_spmd.clone, body=%wide.region_0.3_spmd.clone.sunk | while | flops 562291712 | bytes 28467304 | solution.py:155
  166.6 39.3 %all-gather.31.cloned.1.call-done = bf16[1,1024,1024]{2,1,0:T(8,128)(2,1)} async-done(((bf16[1,64,1024]{2,1,0:T(8,128)(2,1)}), bf16[1,1024,1024]{2,1,0:T(8,128)(2,1)}) %all-gather.31.cloned.1.call-update) | async-done | bytes 2097168 | tf_op jit(solution)/shard_map/all_gather | solution.py:138
  211.8 108.2 %all-gather.33.cloned.1.call-done = bf16[1,1024,4096]{2,1,0:T(8,128)(2,1)} async-done(((bf16[1,64,4096]{2,1,0:T(8,128)(2,1)}), bf16[1,1024,4096]{2,1,0:T(8,128)(2,1)}) %all-gather.33.cloned.1.call-update) | async-done | bytes 8388624 | tf_op jit(solution)/shard_map/all_gather | solution.py:139
  320.0 11.2 fusion.212
  334.5 19.7 %fusion.138 = f32[2,256,4096]{2,1,0:T(8,128)} fusion(f32[2,256,4096]{2,1,0:T(8,128)S(1)} %get-tuple-element.512, f32[4096]{0:T(1024)S(1)} %bitcast.418, u8[256,4096]{1,0:T(8,128)(4,1)S(1)} %get-tuple-element.356, u8[256,4096]{1,0:T(8,128)(4,1)S(1)} %get-tuple-element.355), kind=kLoop, calls=%fused_computation.136 | loop fusion | flops 142606336 | bytes 18890752 | tf_op jit(solution)/shard_map/erfc | solution.py:24
  354.2 79.5 %all-gather.35.cloned.1.call-done = bf16[1,4096,1024]{2,1,0:T(8,128)(2,1)} async-done(((bf16[1,256,1024]{2,1,0:T(8,128)(2,1)}), bf16[1,4096,1024]{2,1,0:T(8,128)(2,1)}) %all-gather.35.cloned.1.call-update) | async-done | bytes 8388624 | tf_op jit(solution)/shard_map/all_gather | solution.py:140
  433.7 10.9 fusion.300
  447.0 81.9 %all-gather.37.cloned.1.call-done = bf16[1,1024,3072]{2,1,0:T(8,128)(2,1)} async-done(((bf16[1,64,3072]{2,1,0:T(8,128)(2,1)}), bf16[1,1024,3072]{2,1,0:T(8,128)(2,1)}) %all-gather.37.cloned.1.call-update) | async-done | bytes 6291472 | tf_op jit(solution)/shard_map/all_gather | solution.py:137
  528.8 6.4 fusion.168
  554.2 8.2 all-gather.27.cloned.1.call-done
  570.6 17.0 %while.61 = (s32[]{:T(128)}, bf16[2,2,256,8,64]{2,4,3,0,1:T(8,128)(2,1)}, f32[2,2,8,256,1]{3,2,1,4,0:T(8,128)S(1)}, f32[2,2,8,256,1]{3,2,1,4,0:T(8,128)S(1)}, bf...) while((s32[]{:T(128)}, ...), condition=%wide.region_11.12_spmd.clone, body=%wide.region_8.11_spmd.clone.sunk | while | flops 562291712 | bytes 28467304 | solution.py:155
  587.6 39.3 %all-gather.39.cloned.1.call-done = bf16[1,1024,1024]{2,1,0:T(8,128)(2,1)} async-done(((bf16[1,64,1024]{2,1,0:T(8,128)(2,1)}), bf16[1,1024,1024]{2,1,0:T(8,128)(2,1)}) %all-gather.39.cloned.1.call-update) | async-done | bytes 2097168 | tf_op jit(solution)/shard_map/all_gather | solution.py:138
  632.7 108.5 %all-gather.41.cloned.1.call-done = bf16[1,1024,4096]{2,1,0:T(8,128)(2,1)} async-done(((bf16[1,64,4096]{2,1,0:T(8,128)(2,1)}), bf16[1,1024,4096]{2,1,0:T(8,128)(2,1)}) %all-gather.41.cloned.1.call-update) | async-done | bytes 8388624 | tf_op jit(solution)/shard_map/all_gather | solution.py:139
  741.2 11.2 fusion.213
  755.6 19.7 %fusion.139 = f32[2,256,4096]{2,1,0:T(8,128)} fusion(f32[2,256,4096]{2,1,0:T(8,128)S(1)} %get-tuple-element.517, f32[4096]{0:T(1024)S(1)} %bitcast.422, u8[256,4096]{1,0:T(8,128)(4,1)S(1)} %get-tuple-element.354, u8[256,4096]{1,0:T(8,128)(4,1)S(1)} %get-tuple-element.353), kind=kLoop, calls=%fused_computation.137 | loop fusion | flops 142606336 | bytes 18890752 | tf_op jit(solution)/shard_map/erfc | solution.py:24
  775.3 79.6 %all-gather.43.cloned.1.call-done = bf16[1,4096,1024]{2,1,0:T(8,128)(2,1)} async-done(((bf16[1,256,1024]{2,1,0:T(8,128)(2,1)}), bf16[1,4096,1024]{2,1,0:T(8,128)(2,1)}) %all-gather.43.cloned.1.call-update) | async-done | bytes 8388624 | tf_op jit(solution)/shard_map/all_gather | solution.py:140
  854.9 13.6 %fusion.302 = (f32[2,256]{1,0:T(2,128)S(1)}, f32[2,256,1024]{2,1,0:T(8,128)S(1)}) fusion(f32[1024]{0:T(1024)S(1)} %bitcast.460, bf16[1,4096,1024]{2,1,0:T(8,128)(2,1)} %all-gather.43.cloned.1.call-done, f32[2,256,4096]{2,1,0:T(8,128)} %fusion.139, f32[2,256,4096]{2,1,0:T(8,128)} %copy-done.22, f32[4096]{0:T(1024)S(1)} %bitcast.423, ...), kind=kOutput, calls=%fused_computation.362 | convolution fusion | flops 4307025408 | bytes 29394944 | tf_op jit(solution)/shard_map/gtd,de->gte/dot_general | solution.py:28
  870.6 16.4 %fusion.303 = (f32[4096]{0:T(1024)}, bf16[2,256,4096]{2,1,0:T(8,128)(2,1)}) fusion(f32[2,256,4096]{2,1,0:T(8,128)} %fusion.139, bf16[1,4096,1024]{2,1,0:T(8,128)(2,1)} %all-gather.43.cloned.1.call-done, f32[2,256]{1,0:T(2,128)S(1)} %negate_multiply_fusion.5, f32[2,256]{1,0:T(2,128)S(1)} %get-tuple-element.508, f32[2,256,1024]{2,1,0:T(8,128)} %copy-done.2, ...), kind=kOutput, calls=%fused_computation.363 | convolution fusion | flops 4333236224 | bytes 32550912 | tf_op jit(solution)/shard_map/gte,de->gtd/dot_general | solution.py:32
  887.0 11.6 fusion.281
  909.1 86.4 %while.62 = (s32[]{:T(128)}, f32[2,2,256,8,64]{2,4,3,0,1:T(8,128)}, bf16[2,2,512,8,64]{2,4,3,0,1:T(8,128)(2,1)}, bf16[2,2,512,8,64]{2,4,3,0,1:T(8,128)(2,1)}, bf...) while((s32[]{:T(128)}, f32[2,2,256,8,64]{2,4,3,0,1:T(8,128)}, ...), condition=%wide.region_22.23_spmd.clone, body=%wide.region_20.22_spmd.clone.sunk | while | flops 1373644800 | bytes 102866048 | solution.py:221
  909.2 6.1 exponential_divide_fusion.4
  919.8 13.4 %bitcast_dynamic-update-slice_fusion.16 = bf16[2,2,512,8,64]{2,4,3,0,1:T(8,128)(2,1)} fusion(bf16[2,2,512,8,64]{2,4,3,0,1:T(8,128)(2,1)} %get-tuple-element.861, s32[]{:T(128)} %get-tuple-element.859, f32[2,8,256,512]{3,2,1,0:T(8,128)} %exponential_divide_fusion.4, f32[2,8,256,512]{3,2,1,0:T(8,128)} %fusion.359, ...), kind=kOutput, calls=%fused_computation.62.clone.1 | convolution fusion | flops 278925824 | bytes 36176896 | tf_op jit(solution)/shard_map/while/body/eval_jaxpr/ghqk,gqhe->gkhe/dot_general | solution.py:81
  933.2 13.9 %fusion.360 = f32[2,2,256,8,64]{2,4,3,0,1:T(8,128)} fusion(f32[2,2,256,8,64]{2,4,3,0,1:T(8,128)} %get-tuple-element.860, s32[]{:T(128)} %get-tuple-element.859, f32[2,8,256,512]{3,2,1,0:T(8,128)} %exponential_divide_fusion.4, f32[2,8,256,512]{3,2,1,0:T(8,128)} %fusion.359, bf16[2,2,512,8,64]{2,4,3,1,0:T(8,128)(2,1)} %get-tuple-element.875), kind=kOutput, calls=%fused_computation.64.clone.1 | convolution fusion | flops 278925824 | bytes 35652608 | tf_op jit(solution)/shard_map/while/body/eval_jaxpr/ghqk,gkhe->gqhe/dot_general | solution.py:78
  947.1 5.2 bitcast_dynamic-update-slice_fusion.17
  952.4 6.1 exponential_divide_fusion.4
  963.0 13.4 %bitcast_dynamic-update-slice_fusion.16 = bf16[2,2,512,8,64]{2,4,3,0,1:T(8,128)(2,1)} fusion(bf16[2,2,512,8,64]{2,4,3,0,1:T(8,128)(2,1)} %get-tuple-element.861, s32[]{:T(128)} %get-tuple-element.859, f32[2,8,256,512]{3,2,1,0:T(8,128)} %exponential_divide_fusion.4, f32[2,8,256,512]{3,2,1,0:T(8,128)} %fusion.359, ...), kind=kOutput, calls=%fused_computation.62.clone.1 | convolution fusion | flops 278925824 | bytes 36176896 | tf_op jit(solution)/shard_map/while/body/eval_jaxpr/ghqk,gqhe->gkhe/dot_general | solution.py:81
  976.4 13.9 %fusion.360 = f32[2,2,256,8,64]{2,4,3,0,1:T(8,128)} fusion(f32[2,2,256,8,64]{2,4,3,0,1:T(8,128)} %get-tuple-element.860, s32[]{:T(128)} %get-tuple-element.859, f32[2,8,256,512]{3,2,1,0:T(8,128)} %exponential_divide_fusion.4, f32[2,8,256,512]{3,2,1,0:T(8,128)} %fusion.359, bf16[2,2,512,8,64]{2,4,3,1,0:T(8,128)(2,1)} %get-tuple-element.875), kind=kOutput, calls=%fused_computation.64.clone.1 | convolution fusion | flops 278925824 | bytes 35652608 | tf_op jit(solution)/shard_map/while/body/eval_jaxpr/ghqk,gkhe->gqhe/dot_general | solution.py:78
  990.3 5.2 bitcast_dynamic-update-slice_fusion.17
  1007.6 13.0 reduce-scatter.7.cloned.1.call-done
  1020.6 9.4 fusion.279
  1030.8 14.8 %fusion.304 = (f32[4096]{0:T(1024)}, bf16[2,256,4096]{2,1,0:T(8,128)(2,1)S(1)}) fusion(f32[2,256,4096]{2,1,0:T(8,128)} %fusion.138, bf16[1,4096,1024]{2,1,0:T(8,128)(2,1)} %all-gather.35.cloned.1.call-done, f32[2,256,1024]{2,1,0:T(8,128)S(1)} %get-tuple-element.460, f32[2,256]{1,0:T(2,128)S(1)} %negate_multiply_fusion.3, f32[2,256,4096]{2,1,0:T(8,128)} %copy-done.21, ...), kind=kOutput, calls=%fused_computation.364 | convolution fusion | flops 4329566208 | bytes 31492096 | tf_op jit(solution)/shard_map/gte,de->gtd/dot_general | solution.py:32
  1045.6 8.1 fusion.280
  1064.4 86.5 %while.63 = (s32[]{:T(128)}, f32[2,2,256,8,64]{2,4,3,0,1:T(8,128)}, bf16[2,2,512,8,64]{2,4,3,0,1:T(8,128)(2,1)}, bf16[2,2,512,8,64]{2,4,3,0,1:T(8,128)(2,1)}, bf...) while((s32[]{:T(128)}, f32[2,2,256,8,64]{2,4,3,0,1:T(8,128)}, ...), condition=%wide.region_31.32_spmd.clone, body=%wide.region_29.31_spmd.clone.sunk | while | flops 1373644800 | bytes 102866048 | solution.py:221
  1064.5 6.1 exponential_divide_fusion.5
  1070.6 4.5 fusion.371
  1075.2 13.4 %bitcast_dynamic-update-slice_fusion.18 = bf16[2,2,512,8,64]{2,4,3,0,1:T(8,128)(2,1)} fusion(bf16[2,2,512,8,64]{2,4,3,0,1:T(8,128)(2,1)} %get-tuple-element.897, s32[]{:T(128)} %get-tuple-element.895, f32[2,8,256,512]{3,2,1,0:T(8,128)} %exponential_divide_fusion.5, f32[2,8,256,512]{3,2,1,0:T(8,128)} %fusion.371, ...), kind=kOutput, calls=%fused_computation.104.clone.1 | convolution fusion | flops 278925824 | bytes 36176896 | tf_op jit(solution)/shard_map/while/body/eval_jaxpr/ghqk,gqhe->gkhe/dot_general | solution.py:81
  1088.6 13.9 %fusion.372 = f32[2,2,256,8,64]{2,4,3,0,1:T(8,128)} fusion(f32[2,2,256,8,64]{2,4,3,0,1:T(8,128)} %get-tuple-element.896, s32[]{:T(128)} %get-tuple-element.895, f32[2,8,256,512]{3,2,1,0:T(8,128)} %exponential_divide_fusion.5, f32[2,8,256,512]{3,2,1,0:T(8,128)} %fusion.371, bf16[2,2,512,8,64]{2,4,3,1,0:T(8,128)(2,1)} %get-tuple-element.911), kind=kOutput, calls=%fused_computation.106.clone.1 | convolution fusion | flops 278925824 | bytes 35652608 | tf_op jit(solution)/shard_map/while/body/eval_jaxpr/ghqk,gkhe->gqhe/dot_general | solution.py:78
  1102.5 5.2 bitcast_dynamic-update-slice_fusion.19
  1107.8 6.1 exponential_divide_fusion.5
  1113.9 4.5 fusion.371
  1118.4 13.4 %bitcast_dynamic-update-slice_fusion.18 = bf16[2,2,512,8,64]{2,4,3,0,1:T(8,128)(2,1)} fusion(bf16[2,2,512,8,64]{2,4,3,0,1:T(8,128)(2,1)} %get-tuple-element.897, s32[]{:T(128)} %get-tuple-element.895, f32[2,8,256,512]{3,2,1,0:T(8,128)} %exponential_divide_fusion.5, f32[2,8,256,512]{3,2,1,0:T(8,128)} %fusion.371, ...), kind=kOutput, calls=%fused_computation.104.clone.1 | convolution fusion | flops 278925824 | bytes 36176896 | tf_op jit(solution)/shard_map/while/body/eval_jaxpr/ghqk,gqhe->gkhe/dot_general | solution.py:81
  1131.8 13.9 %fusion.372 = f32[2,2,256,8,64]{2,4,3,0,1:T(8,128)} fusion(f32[2,2,256,8,64]{2,4,3,0,1:T(8,128)} %get-tuple-element.896, s32[]{:T(128)} %get-tuple-element.895, f32[2,8,256,512]{3,2,1,0:T(8,128)} %exponential_divide_fusion.5, f32[2,8,256,512]{3,2,1,0:T(8,128)} %fusion.371, bf16[2,2,512,8,64]{2,4,3,1,0:T(8,128)(2,1)} %get-tuple-element.911), kind=kOutput, calls=%fused_computation.106.clone.1 | convolution fusion | flops 278925824 | bytes 35652608 | tf_op jit(solution)/shard_map/while/body/eval_jaxpr/ghqk,gkhe->gqhe/dot_general | solution.py:78
  1145.7 5.2 bitcast_dynamic-update-slice_fusion.19
  1178.9 7.8 add_convert_fusion
  1186.8 133.1 %all-reduce.3.cloned.1.call-done = (f32[1,1024]{1,0:T(1,128)}, f32[1,1024]{1,0:T(1,128)}, f32[1,1024]{1,0:T(1,128)}, f32[1,1024]{1,0:T(1,128)}, f32[1,1024]{1,0:...) async-done(((f32[1,1024]{1,0:T(1,128)}, f32[1,1024]{1,0:T(1,128)}, ...) | async-done | bytes 81936 | tf_op jit(solution)/shard_map/psum | solution.py:253
  (319 shorter events, 195.0 us)
Async XLA Ops:
  7.2 101.1 %all-gather.29.cloned.1.call-start = ((), (), s32[]{:S(2)}) async-start(), calls=%async_computation.12 | async-start | bytes 6684672 | tf_op jit(solution)/shard_map/all_gather | solution.py:137
  9.3 120.9 %all-gather.21.cloned.1.call-start = ((), (), s32[]{:S(2)}) async-start(), calls=%async_computation.4 | async-start | bytes 3145728 | tf_op jit(solution)/shard_map/all_gather | solution.py:150
  118.4 22.9 %all-gather.23.cloned.1.call-start = ((), (), s32[]{:S(2)}) async-start(), calls=%async_computation.5 | async-start | bytes 3145728 | tf_op jit(solution)/shard_map/all_gather | solution.py:149
  121.2 84.7 %all-gather.31.cloned.1.call-start = ((), (), s32[]{:S(2)}) async-start(), calls=%async_computation.13 | async-start | bytes 2228224 | tf_op jit(solution)/shard_map/all_gather | solution.py:138
  122.0 198.0 %all-gather.33.cloned.1.call-start = ((), (), s32[]{:S(2)}) async-start(), calls=%async_computation.14 | async-start | bytes 8912896 | tf_op jit(solution)/shard_map/all_gather | solution.py:139
  123.2 310.5 %all-gather.35.cloned.1.call-start = ((), (), s32[]{:S(2)}) async-start(), calls=%async_computation.15 | async-start | bytes 8912896 | tf_op jit(solution)/shard_map/all_gather | solution.py:140
  124.3 404.5 %all-gather.37.cloned.1.call-start = ((), (), s32[]{:S(2)}) async-start(), calls=%async_computation.16 | async-start | bytes 6684672 | tf_op jit(solution)/shard_map/all_gather | solution.py:137
  125.1 423.4 %all-gather.25.cloned.1.call-start = ((), (), s32[]{:S(2)}) async-start(), calls=%async_computation.6 | async-start | bytes 3145728 | tf_op jit(solution)/shard_map/all_gather | solution.py:150
  126.5 307.2 %copy-start.36 = (f32[1,4096]{1,0:T(1,128)}, f32[1,4096]{1,0:T(1,128)S(1)}, u32[]{:S(2)}) copy-start(f32[1,4096]{1,0:T(1,128)S(1)} %get-tuple-element.489) | copy-start | bytes 49156
  127.1 306.6 %copy-start.55 = (f32[1,1024]{1,0:T(1,128)}, f32[1,1024]{1,0:T(1,128)S(1)}, u32[]{:S(2)}) copy-start(f32[1,1024]{1,0:T(1,128)S(1)} %get-tuple-element.497) | copy-start | bytes 12292
  129.0 497.9 %copy-start.57 = (f32[1,1024]{1,0:T(1,128)}, f32[1,1024]{1,0:T(1,128)S(1)}, u32[]{:S(2)}) copy-start(f32[1,1024]{1,0:T(1,128)S(1)} %get-tuple-element.491) | copy-start | bytes 12292
  134.2 15.4 %copy-start.33 = (s32[2]{0:T(128)S(1)}, s32[2]{0:T(128)}, u32[]{:S(2)}) copy-start(s32[2]{0:T(128)} %param.28) | copy-start | bytes 28
  166.6 164.6 %copy-start = (bf16[2,2,512,8,64]{2,4,3,1,0:T(8,128)(2,1)}, bf16[2,2,512,8,64]{2,4,3,1,0:T(8,128)(2,1)S(1)}, u32[]{:S(2)}) copy-start(bf16[2,2,512,8,64]{2,4,3,1,0:T(8,128)(2,1)S(1)} %get-tuple-element.963) | copy-start | bytes 6291460
  166.6 164.6 %copy-start.6 = (bf16[2,2,256,8,64]{2,4,3,1,0:T(8,128)(2,1)}, bf16[2,2,256,8,64]{2,4,3,1,0:T(8,128)(2,1)S(1)}, u32[]{:S(2)}) copy-start(bf16[2,2,256,8,64]{2,4,3,1,0:T(8,128)(2,1)S(1)} %get-tuple-element.967) | copy-start | bytes 3145732
  166.6 164.6 %copy-start.28 = (f32[2,2,8,256,1]{3,2,1,4,0:T(8,128)}, f32[2,2,8,256,1]{3,2,1,4,0:T(8,128)S(1)}, u32[]{:S(2)}) copy-start(f32[2,2,8,256,1]{3,2,1,4,0:T(8,128)S(1)} %get-tuple-element.889) | copy-start | bytes 98308
  166.6 164.6 %copy-start.30 = (f32[2,2,8,256,1]{3,2,1,4,0:T(8,128)}, f32[2,2,8,256,1]{3,2,1,4,0:T(8,128)S(1)}, u32[]{:S(2)}) copy-start(f32[2,2,8,256,1]{3,2,1,4,0:T(8,128)S(1)} %get-tuple-element.890) | copy-start | bytes 98308
  209.6 224.1 %copy-start.46 = (f32[2,256]{1,0:T(2,128)}, f32[2,256]{1,0:T(2,128)S(1)}, u32[]{:S(2)}) copy-start(f32[2,256]{1,0:T(2,128)S(1)} %broadcast_multiply_fusion.3) | copy-start | bytes 6148
  211.8 221.9 %copy-start.60 = (f32[2,256]{1,0:T(2,128)}, f32[2,256]{1,0:T(2,128)S(1)}, u32[]{:S(2)}) copy-start(f32[2,256]{1,0:T(2,128)S(1)} %fusion.270) | copy-start | bytes 6148
  334.4 99.3 %copy-start.11 = (f32[2,256,1024]{2,1,0:T(8,128)S(1)}, f32[2,256,1024]{2,1,0:T(8,128)}, u32[]{:S(2)}) copy-start(f32[2,256,1024]{2,1,0:T(8,128)} %copy-done.10) | copy-start | bytes 6291460
  444.7 182.2 %copy-start.48 = (f32[2,256]{1,0:T(2,128)}, f32[2,256]{1,0:T(2,128)S(1)}, u32[]{:S(2)}) copy-start(f32[2,256]{1,0:T(2,128)S(1)} %broadcast_multiply_fusion.2) | copy-start | bytes 6148
  447.0 179.9 %copy-start.62 = (f32[2,256]{1,0:T(2,128)}, f32[2,256]{1,0:T(2,128)S(1)}, u32[]{:S(2)}) copy-start(f32[2,256]{1,0:T(2,128)S(1)} %fusion.271) | copy-start | bytes 6148
  539.4 22.9 %all-gather.27.cloned.1.call-start = ((), (), s32[]{:S(2)}) async-start(), calls=%async_computation.7 | async-start | bytes 3145728 | tf_op jit(solution)/shard_map/all_gather | solution.py:149
  542.2 84.7 %all-gather.39.cloned.1.call-start = ((), (), s32[]{:S(2)}) async-start(), calls=%async_computation.17 | async-start | bytes 2228224 | tf_op jit(solution)/shard_map/all_gather | solution.py:138
  542.8 198.4 %all-gather.41.cloned.1.call-start = ((), (), s32[]{:S(2)}) async-start(), calls=%async_computation.18 | async-start | bytes 8912896 | tf_op jit(solution)/shard_map/all_gather | solution.py:139
  543.6 311.3 %all-gather.43.cloned.1.call-start = ((), (), s32[]{:S(2)}) async-start(), calls=%async_computation.19 | async-start | bytes 8912896 | tf_op jit(solution)/shard_map/all_gather | solution.py:140
  544.1 463.4 %reduce-scatter.5.cloned.1.call-start = ((), (), s32[]{:S(2)}) async-start(), calls=%async_computation.8 | async-start | bytes 3145728 | tf_op jit(solution)/shard_map/reduce_scatter | solution.py:226
  570.6 56.3 %copy-start.74 = (f32[1,1024]{1,0:T(1,128)S(1)}, f32[1,1024]{1,0:T(1,128)}, u32[]{:S(2)}) copy-start(f32[1,1024]{1,0:T(1,128)} %get-tuple-element.500) | copy-start | bytes 12292
  587.6 45.1 %copy-start.7 = (bf16[2,2,256,8,64]{2,4,3,1,0:T(8,128)(2,1)}, bf16[2,2,256,8,64]{2,4,3,1,0:T(8,128)(2,1)S(1)}, u32[]{:S(2)}) copy-start(bf16[2,2,256,8,64]{2,4,3,1,0:T(8,128)(2,1)S(1)} %get-tuple-element.968) | copy-start | bytes 3145732
  626.9 114.3 %copy-start.38 = (f32[1,4096]{1,0:T(1,128)S(1)}, f32[1,4096]{1,0:T(1,128)}, u32[]{:S(2)}) copy-start(f32[1,4096]{1,0:T(1,128)} %get-tuple-element.488) | copy-start | bytes 49156
  626.9 114.3 %copy-start.59 = (f32[1,1024]{1,0:T(1,128)S(1)}, f32[1,1024]{1,0:T(1,128)}, u32[]{:S(2)}) copy-start(f32[1,1024]{1,0:T(1,128)} %get-tuple-element.496) | copy-start | bytes 12292
  626.9 114.3 %copy-start.72 = (f32[1,1024]{1,0:T(1,128)S(1)}, f32[1,1024]{1,0:T(1,128)}, u32[]{:S(2)}) copy-start(f32[1,1024]{1,0:T(1,128)} %get-tuple-element.498) | copy-start | bytes 12292
  755.6 99.3 %copy-start.73 = (f32[1,1024]{1,0:T(1,128)S(1)}, f32[1,1024]{1,0:T(1,128)}, u32[]{:S(2)}) copy-start(f32[1,1024]{1,0:T(1,128)} %get-tuple-element.494) | copy-start | bytes 12292
  868.5 18.5 %copy-start.40 = (f32[2,256]{1,0:T(2,128)}, f32[2,256]{1,0:T(2,128)S(1)}, u32[]{:S(2)}) copy-start(f32[2,256]{1,0:T(2,128)S(1)} %broadcast_multiply_fusion) | copy-start | bytes 6148
  869.2 17.8 %copy-start.42 = (f32[2,256]{1,0:T(2,128)}, f32[2,256]{1,0:T(2,128)S(1)}, u32[]{:S(2)}) copy-start(f32[2,256]{1,0:T(2,128)S(1)} %get-tuple-element.508) | copy-start | bytes 6148
  869.2 17.8 %copy-start.44 = (f32[2,256]{1,0:T(2,128)}, f32[2,256]{1,0:T(2,128)S(1)}, u32[]{:S(2)}) copy-start(f32[2,256]{1,0:T(2,128)S(1)} %get-tuple-element.509) | copy-start | bytes 6148
  870.6 16.4 %copy-start.64 = (f32[2,256]{1,0:T(2,128)}, f32[2,256]{1,0:T(2,128)S(1)}, u32[]{:S(2)}) copy-start(f32[2,256]{1,0:T(2,128)S(1)} %negate_multiply_fusion.5) | copy-start | bytes 6148
  999.6 21.0 %copy-start.49 = (f32[2,256]{1,0:T(2,128)S(1)}, f32[2,256]{1,0:T(2,128)}, u32[]{:S(2)}) copy-start(f32[2,256]{1,0:T(2,128)} %copy-done.48) | copy-start | bytes 6148
  999.6 21.0 %copy-start.58 = (f32[1,1024]{1,0:T(1,128)S(1)}, f32[1,1024]{1,0:T(1,128)}, u32[]{:S(2)}) copy-start(f32[1,1024]{1,0:T(1,128)} %copy-done.57) | copy-start | bytes 12292
  999.6 20.9 %reduce-scatter.7.cloned.1.call-start = ((), (), s32[]{:S(2)}) async-start(), calls=%async_computation.9 | async-start | bytes 3145728 | tf_op jit(solution)/shard_map/reduce_scatter | solution.py:229
  1003.7 172.9 %reduce-scatter.11.cloned.1.call-start = ((), (), s32[]{:S(2)}) async-start(), calls=%async_computation.11 | async-start | bytes 3145728 | tf_op jit(solution)/shard_map/reduce_scatter | solution.py:229
  1005.4 24.6 %copy-start.53 = (f32[2,256]{1,0:T(2,128)S(1)}, f32[2,256]{1,0:T(2,128)}, u32[]{:S(2)}) copy-start(f32[2,256]{1,0:T(2,128)} %copy-done.52) | copy-start | bytes 6148
  1005.4 24.6 %copy-start.14 = (f32[2,256,1024]{2,1,0:T(8,128)S(1)}, f32[2,256,1024]{2,1,0:T(8,128)}, u32[]{:S(2)}) copy-start(f32[2,256,1024]{2,1,0:T(8,128)} %copy-done.13) | copy-start | bytes 6291460
  1005.4 24.6 %copy-start.63 = (f32[2,256]{1,0:T(2,128)S(1)}, f32[2,256]{1,0:T(2,128)}, u32[]{:S(2)}) copy-start(f32[2,256]{1,0:T(2,128)} %copy-done.62) | copy-start | bytes 6148
  1030.7 14.8 %copy-start.18 = (f32[2,256,1024]{2,1,0:T(8,128)}, f32[2,256,1024]{2,1,0:T(8,128)S(1)}, u32[]{:S(2)}) copy-start(f32[2,256,1024]{2,1,0:T(8,128)S(1)} %get-tuple-element.460) | copy-start | bytes 6291460
  1030.7 14.8 %copy-start.12 = (f32[2,256,1024]{2,1,0:T(8,128)S(1)}, f32[2,256,1024]{2,1,0:T(8,128)}, u32[]{:S(2)}) copy-start(f32[2,256,1024]{2,1,0:T(8,128)} %copy-done.10) | copy-start | bytes 6291460
  1030.7 14.8 %copy-start.47 = (f32[2,256]{1,0:T(2,128)S(1)}, f32[2,256]{1,0:T(2,128)}, u32[]{:S(2)}) copy-start(f32[2,256]{1,0:T(2,128)} %copy-done.46) | copy-start | bytes 6148
  1155.0 24.0 %reduce-scatter.9.cloned.1.call-start = ((), (), s32[]{:S(2)}) async-start(), calls=%async_computation.10 | async-start | bytes 3145728 | tf_op jit(solution)/shard_map/reduce_scatter | solution.py:226
  1159.2 160.7 %all-reduce.3.cloned.1.call-start = ((), (), s32[]{:S(2)}) async-start(), calls=%async_computation.20 | async-start | bytes 163840 | tf_op jit(solution)/shard_map/psum | solution.py:253
  (46 other events, 311.3 us)
Sparse Core Ops, SparseCore 0:
  11.4 96.8 all-gather.28
  118.6 8.8 all-gather.20
  129.6 11.7 all-gather.22
  144.0 61.8 all-gather.30
  208.5 111.4 all-gather.32
  322.6 111.0 all-gather.34
  436.5 92.3 all-gather.36
  539.6 8.8 all-gather.24
  550.6 11.7 all-gather.26
  565.0 61.8 all-gather.38
  629.7 111.4 all-gather.40
  743.8 111.0 all-gather.42
  999.7 7.7 reduce-scatter.4
  1009.7 10.7 reduce-scatter.6
  1155.1 10.7 reduce-scatter.10
  1168.1 10.7 reduce-scatter.8
  1186.4 133.4 all-reduce.2
where the time goes:
time: 1340 us; the launch traced here: 1330 us
  waiting for transfers between devices  800 us (60%)
  matrix products  337 us (25%)
  local copies, waits for them, and re-layouts  99.8 us (7%)
  other arithmetic  78.7 us (6%)
  between operations  15 us (1%)
    all_gather x2, waiting for transfers between devices, on_device(): lax.all_gather(inner_weight[layer_index], 'batch', axis=0, tiled=True)  217 us
    all_gather x2, waiting for transfers between devices, on_device(): lax.all_gather(projection_weight[layer_index], 'batch', axis=0, tiled=True)  178 us
    all_gather x2, waiting for transfers between devices, on_device(): lax.all_gather(outer_weight[layer_index], 'batch', axis=0, tiled=True)  159 us
    psum x1, waiting for transfers between devices, on_device(): lax.psum((local_terms[0], local_terms[1], local_terms[2], local_terms[3],...  133 us
    all_gather x2, waiting for transfers between devices, on_device(): lax.all_gather(output_weight[layer_index], 'batch', axis=0, tiled=True)  78.6 us
    dot_general x8, matrix products, project_back(): jnp.einsum('gte,de->gtd', grad_rows, weight, preferred_element_type=jnp.f...  72.6 us
    dot_general x8, matrix products, project(): jnp.einsum('gtd,de->gte', left, weight, preferred_element_type=jnp.float32)  66.9 us
    dot_general x4, matrix products, attend_back(): jnp.einsum('ghqk,gkhe->gqhe', grad_scores, key_block, preferred_element_t...  55.5 us
  transfers between devices with their start and end apart: 17, of which 15 were waited for; matrix products, arithmetic and copies ran while one was open for 15% of the time, Pallas kernels for 0%

commit v1 on v0

v1 whole, which is shorter than its diff:
```python
import functools

import jax
import jax.numpy as jnp
from jax import lax
from jax.experimental import pallas as pl
from jax.experimental.pallas import tpu as pltpu
from jax.sharding import PartitionSpec as P

D = 1024
HEADS = 16
HEAD = 64
FF = 4096
LAYERS = 2
UNITS = 24
PER = 12
SPLIT = 640
BLK = 256
ROWS = 64
EPSILON = 1e-12
MASKED = -1000000000.0
MESH = pl.DeviceIdType.MESH
BF = jnp.bfloat16
F32 = jnp.float32


def sizes(batch):
    side = 2 ** ((batch.bit_length() - 1) // 3)
    return batch // (side * side), side


def lane(n):
    return 1 if n == 2 else 2 * (n - 1)


class Comm:
    def __init__(self, nz, n, gathered, ssem, rsem, sib_s, sib_r, slots, gap):
        self.nz, self.n, self.G = nz, n, gathered
        self.ssem, self.rsem, self.sib_s, self.sib_r = ssem, rsem, sib_s, sib_r
        self.slots, self.gap = slots, gap
        self.b = lax.axis_index("batch")
        self.c = lax.axis_index("blk")
        self.z, self.y, self.x = self.b // (n * n), (self.b // n) % n, self.b % n
        self.stages = 1 + (n - 1) + (nz - 1) + (n - 1)
        self.fbase = 2 * (nz - 1)

    @staticmethod
    def sems(nz, n):
        return 2 * (nz - 1) + 2 * nz * lane(n)

    def cols(self, core):
        return pl.ds(0, SPLIT) if core == 0 else pl.ds(SPLIT, D - SPLIT)

    def setup(self, core, par, u):
        first_x = (core == 0) == (par == 0)
        cs, g, n = self.cols(core), self.G, self.n
        self.f, self.s = (self.x, self.y) if first_x else (self.y, self.x)
        self.fstr, self.sstr = (1, n) if first_x else (n, 1)
        if first_x:
            self.sl = lambda zi, fi, si: g.at[u, zi, si, fi, :, cs]
        else:
            self.sl = lambda zi, fi, si: g.at[u, zi, fi, si, :, cs]
        self.slot = u % self.slots

    def copy(self, ref, idx, to):
        return pltpu.make_async_remote_copy(
            src_ref=ref,
            dst_ref=ref,
            send_sem=self.ssem.at[self.slot, idx],
            recv_sem=self.rsem.at[self.slot, idx],
            device_id=(to, self.c),
            device_id_type=MESH,
        )

    def dirs(self, length):
        return (0,) if length == 2 else (0, 1)

    def act(self, cp, mode):
        if mode == "start":
            cp.start()
        else:
            cp.wait_send()

    def arrive(self, ref, base, pos, length, stride, j, e, mode):
        if length == 2:
            to = self.b + stride * (1 - 2 * pos)
            if j == 0:
                self.act(self.copy(ref(pos), base, to), mode)
            elif mode == "start":
                self.copy(ref(1 - pos), base, to).wait_recv()
            return
        if j == 0:
            for d in (0, 1):

                @pl.when((pos + 1 < length) if d == 0 else (pos >= 1))
                def _():
                    self.act(self.copy(ref(pos), base + d, self.b + (stride if d == 0 else -stride)), mode)

            return
        src = pos - j if e == 0 else pos + j
        ok = (src >= 0) if e == 0 else (src < length)
        fwd = (pos + 1 < length) if e == 0 else (pos >= 1)
        to = self.b + (stride if e == 0 else -stride)
        if mode == "start":

            @pl.when(ok)
            def _():
                self.copy(ref(src), base + 2 * (j - 1) + e, to).wait_recv()

        if j < length - 1:

            @pl.when(ok & fwd)
            def _():
                self.act(self.copy(ref(src), base + 2 * j + e, to), mode)

    def hops(self):
        yield 0, 0
        for h in range(1, self.nz):
            for d in (0, 1):
                yield h, d

    def run(self, core, par, u, k, mode):
        self.setup(core, par, u)
        n, nz, z, b = self.n, self.nz, self.z, self.b
        lw = lane(n)
        sbase = self.fbase + nz * lw
        f, s = self.f, self.s
        pre = 0
        if core == 0:
            for j in range(n):
                if k is None or k == j:
                    for e in self.dirs(n) if j else (0,):
                        self.arrive(lambda i: self.sl(z, i, s), self.fbase, f, n, self.fstr, j, e, mode)
            pre = n - 1
        last = (n - 1) if core == 0 else 2 * (n - 1)
        for h, d in self.hops():
            zi = z - h if d == 0 else z + h
            fi = f if core == 1 else slice(None)

            def along_z():
                ref = self.sl(zi, fi, s)
                if h and mode == "start":
                    self.copy(ref, 2 * (h - 1) + d, b).wait_recv()
                if h < nz - 1:
                    for dd in (0, 1) if h == 0 else (d,):

                        @pl.when((z + 1 < nz) if dd == 0 else (z >= 1))
                        def _():
                            self.act(self.copy(ref, 2 * h + dd, b + (n * n if dd == 0 else -n * n)), mode)

            def in_plane(step):
                q = step
                if core == 1:
                    if step < n:
                        for e in self.dirs(n) if step else (0,):
                            self.arrive(
                                lambda i: self.sl(zi, i, s), self.fbase + zi * lw, f, n, self.fstr, step, e, mode
                            )
                    q = step - (n - 1)
                if q >= 0:
                    for e in self.dirs(n) if q else (0,):
                        self.arrive(
                            lambda i: self.sl(zi, slice(None), i), sbase + zi * lw, s, n, self.sstr, q, e, mode
                        )

            def events():
                for step in range(last + 1):
                    if k is None or k == pre + h + step:
                        if step == 0:
                            along_z()
                        in_plane(step)

            if k is None or 0 <= k - pre - h <= last:
                if h == 0:
                    events()
                else:
                    pl.when((zi >= 0) if d == 0 else (zi < nz))(events)
        if k == self.stages - 1:
            self.sibling(core, u).start()
        if k is None:
            self.sibling(core, u).wait_send()

    def sibling(self, core, u):
        ref = self.G.at[u, :, :, :, :, self.cols(core)]
        return pltpu.make_async_remote_copy(
            src_ref=ref,
            dst_ref=ref,
            send_sem=self.sib_s.at[u % self.slots],
            recv_sem=self.sib_r.at[u],
            device_id=(self.b, 1 - self.c),
            device_id_type=MESH,
        )

    def tick(self, t):
        for core in (0, 1):

            @pl.when(self.c == core)
            def _():
                for k in [self.stages, *reversed(range(self.stages))]:
                    u = t - k * self.gap
                    for par in (0, 1):

                        @pl.when((u >= 0) & (u < UNITS) & (u % 2 == par))
                        def _():
                            if k == self.stages:
                                self.run(core, par, u, None, "drain")
                            else:
                                self.run(core, par, u, k, "start")

    def partners(self):
        yield (self.b, 1 - self.c)
        step = 1
        while step < self.nz * self.n * self.n:
            yield (self.b + step * (1 - 2 * ((self.b // step) % 2)), self.c)
            step *= 2

    def barrier(self):
        bar = pltpu.get_barrier_semaphore()
        n, nz = self.n, self.nz
        total = jnp.int32(0)
        for to in self.partners():
            pl.semaphore_signal(bar, inc=1, device_id=to, device_id_type=MESH)
            total = total + 1
        for length, pos, stride in ((n, self.x, 1), (n, self.y, n), (nz, self.z, n * n)):
            for d in (0, 1):
                ok = (pos + 1 < length) if d == 0 else (pos >= 1)
                total = total + ok.astype(jnp.int32)

                @pl.when(ok)
                def _():
                    to = (self.b + (stride if d == 0 else -stride), self.c)
                    pl.semaphore_signal(bar, inc=1, device_id=to, device_id_type=MESH)

        pl.semaphore_wait(bar, total)


def dot(a, b, ca=1, cb=0):
    return lax.dot_general(a, b, (((ca,), (cb,)), ((), ())), preferred_element_type=F32)


def fold(values):
    rows, cols = values.shape
    return jnp.sum(values.reshape(rows // 8, 8, cols), axis=0)


def colsum(values):
    return jnp.sum(values, axis=0, keepdims=True)


def kernel(
    nz,
    n,
    gap,
    slots,
    lengths,
    separators,
    hidden,
    cotangent,
    type_table,
    proj,
    outw,
    inner,
    outer,
    query_bias,
    value_bias,
    output_bias,
    inner_bias,
    outer_bias,
    first_gain,
    first_shift,
    second_gain,
    second_shift,
    layer_output,
    input_gradient,
    grads,
    G,
    P0,
    stg,
    xin,
    cot,
    xs,
    xb,
    qkv,
    qT,
    prob,
    mid,
    act,
    gp,
    n1,
    n2,
    r1,
    r2,
    gcT,
    dkT,
    dvT,
    wbuf,
    bg,
    arb,
    dqs8,
    ssem,
    rsem,
    sib_s,
    sib_r,
    lsem,
    wsem,
    xsem,
    psem,
    osem,
    asem,
):
    nb = nz * n * n
    R = D // nb
    T = xs.shape[0]
    half = T // 2
    quarter = nb // 4
    comm = Comm(nz, n, G, ssem, rsem, sib_s, sib_r, slots, gap)
    c = comm.c
    other = (comm.b, 1 - c)
    ctx = xin

    def stage_in(op):
        for l in range(LAYERS):
            for u in range(8):
                m, j = (proj, u) if u < 3 else (outw, 0) if u == 3 else (inner, u - 4)
                cp = pltpu.make_async_copy(m.at[l, :, pl.ds(j * D, D)], stg.at[l * PER + u], lsem.at[l * PER + u])
                getattr(cp, op)()
            for j in range(4):
                for g in range(4):
                    cp = pltpu.make_async_copy(
                        outer.at[l, pl.ds(g * R, R), pl.ds(j * BLK, BLK)],
                        stg.at[l * PER + 8 + j, :, pl.ds(g * BLK, BLK)],
                        lsem.at[UNITS + (l * 4 + j) * 4 + g],
                    )
                    getattr(cp, op)()

    def place(op):
        for core in (0, 1):

            @pl.when(c == core)
            def _():
                def one(u, carry):
                    cs = comm.cols(core)
                    cp = pltpu.make_async_copy(
                        stg.at[u, :, cs], G.at[u, comm.z, comm.y, comm.x, :, cs], lsem.at[u]
                    )
                    getattr(cp, op)()
                    return carry

                lax.fori_loop(0, UNITS, one, 0)

    def exchange(op):
        for i, (src, dst) in enumerate(((hidden, xin), (cotangent, cot))):
            rows = pl.ds(pl.multiple_of(c * half, half), half)
            lc = pltpu.make_async_copy(src.at[c], dst.at[rows], xsem.at[3 * i])
            rc = pltpu.make_async_remote_copy(
                src_ref=src.at[1 - c],
                dst_ref=dst.at[rows],
                send_sem=xsem.at[3 * i + 1],
                recv_sem=xsem.at[3 * i + 2],
                device_id=other,
                device_id_type=MESH,
            )
            getattr(lc, op)()
            getattr(rc, op)()

    stage_in("start")
    comm.barrier()
    exchange("start")
    stage_in("wait")
    place("start")
    place("wait")

    def row(ref, l):
        return ref[pl.ds(l, 1), :]

    def cols(i, width=BLK):
        return pl.ds(pl.multiple_of(i * width, width), width)

    lanes = lax.broadcasted_iota(jnp.int32, (T, 2 * HEAD), 1)
    halves = (lanes < HEAD, lanes >= HEAD)

    def init_x():
        exchange("wait")
        t0 = type_table[0:1, :].astype(F32)
        t1 = type_table[1:2, :].astype(F32)
        sep = separators[c]

        def rows_of(i, carry):
            rs = pl.ds(pl.multiple_of(i * ROWS, ROWS), ROWS)
            at = i * ROWS + lax.broadcasted_iota(jnp.int32, (ROWS, D), 0)
            second = (at > sep).astype(F32)
            x = xin[rs, :].astype(F32) + t0 + second * (t1 - t0)
            xs[rs, :] = x
            xb[rs, :] = x.astype(BF)
            return carry

        lax.fori_loop(0, T // ROWS, rows_of, 0)

    def load_unit(u, slot, op):
        def one(g, carry):
            cp = pltpu.make_async_copy(
                G.at[u, :, :, :, :, cols(g)], wbuf.at[slot, :, :, :, g], wsem.at[slot, g]
            )
            getattr(cp, op)()
            return carry

        lax.fori_loop(0, 4, one, 0)

    def load_rows(l, f, slot, op):
        zs = pl.ds(f * (nz // 4), nz // 4)

        def one(i, carry):
            j, g = i // 4, i % 4
            cp = pltpu.make_async_copy(
                G.at[l * PER + 8 + j, zs, :, :, :, cols(g)],
                wbuf.at[slot, pl.ds(j * (nz // 4), nz // 4), :, :, g],
                wsem.at[slot, i],
            )
            getattr(cp, op)()
            return carry

        lax.fori_loop(0, 16, one, 0)

    def w_cols(slot, g):
        return wbuf[slot, :, :, :, g].reshape(D, BLK)

    def w_rows(slot, i):
        q = nz // 4
        return jnp.concatenate(
            [wbuf[slot, pl.ds(i * q, q), :, :, g].reshape(BLK, BLK) for g in range(4)], axis=1
        )

    def o_rows(slot, i):
        if nz == 4:
            parts = [wbuf[slot, j, i // n, i % n].reshape(BLK, BLK) for j in range(4)]
        else:
            q = nz // 4
            parts = [wbuf[slot, pl.ds(j * q, q)].reshape(D, BLK)[i * BLK : (i + 1) * BLK] for j in range(4)]
        return jnp.concatenate(parts, axis=1)

    def norm_rows(z, gain, shift):
        average = jnp.mean(z, axis=1, keepdims=True)
        centred = z - average
        r = lax.rsqrt(jnp.mean(centred * centred, axis=1, keepdims=True) + EPSILON)
        normed = centred * r
        return normed, r, normed * gain + shift

    def do_qkv(l, j, slot):
        is_q, is_v = (j == 0).astype(F32), (j == 2).astype(F32)
        at = jnp.where(j == 0, 0, 2 * l + j)
        for g in range(4):
            sl = slice(g * BLK, (g + 1) * BLK)
            bias = query_bias[pl.ds(l, 1), sl] * is_q + value_bias[pl.ds(l, 1), sl] * is_v
            qkv[at, :, sl] = (dot(xb[...], w_cols(slot, g)) + bias).astype(BF)

    def do_attention(l, lo, hi):
        key_ok = lax.broadcasted_iota(jnp.int32, (1, T), 1) < lengths[c]

        def pair(hp, carry):
            cs = cols(hp, 2 * HEAD)
            q2, k2, v2 = qkv[0, :, cs], qkv[2 * l + 1, :, cs], qkv[2 * l + 2, :, cs]
            outs = []
            for hh in (0, 1):
                qm = jnp.where(halves[hh], q2 * BF(HEAD**-0.5), BF(0))
                s = jnp.where(key_ok, dot(qm, k2, 1, 1), MASKED)
                e = jnp.exp(s - jnp.max(s, axis=1, keepdims=True))
                p = (e * (1.0 / jnp.sum(e, axis=1, keepdims=True))).astype(BF)
                prob[2 * hp + hh] = p
                outs.append(dot(p, v2))
            ctx[:, cs] = jnp.where(halves[0], outs[0], outs[1]).astype(BF)
            qT[l, cs, :] = q2.T
            return carry

        lax.fori_loop(lo, hi, pair, 0)

    def do_out(l, slot):
        for g in range(4):
            sl = slice(g * BLK, (g + 1) * BLK)
            mid[:, sl] = xs[:, sl] + dot(ctx[...], w_cols(slot, g)) + output_bias[pl.ds(l, 1), sl]
        gain, shift = row(first_gain, l), row(first_shift, l)

        def rows_of(i, carry):
            rs = pl.ds(pl.multiple_of(i * ROWS, ROWS), ROWS)
            normed, r, y = norm_rows(mid[rs, :], gain, shift)
            n1[l, rs, :] = normed.astype(BF)
            r1[l, rs, :] = r
            mid[rs, :] = y
            xb[rs, :] = y.astype(BF)
            return carry

        lax.fori_loop(0, T // ROWS, rows_of, 0)

    def do_inner(l, i, slot):
        for g in range(4):
            cs = cols(i * 4 + g)
            h = dot(xb[...], w_cols(slot, g)) + inner_bias[pl.ds(l, 1), cs]
            cdf = 0.5 + 0.5 * lax.erf(h * (0.5**0.5))
            act[:, cs] = (h * cdf).astype(BF)
            gp[l, :, cs] = (cdf + h * (jnp.exp(-0.5 * h * h) * 0.3989422804014327)).astype(BF)

    def do_outer(l, j, slot):
        cs = cols(j)
        w = wbuf[slot].reshape(FF, BLK)
        xs[:, cs] = mid[:, cs] + dot(act[...], w) + outer_bias[pl.ds(l, 1), cs]

    def do_norm2(l):
        gain, shift = row(second_gain, l), row(second_shift, l)

        def rows_of(i, carry):
            rs = pl.ds(pl.multiple_of(i * ROWS, ROWS), ROWS)
            normed, r, y = norm_rows(xs[rs, :], gain, shift)
            n2[l, rs, :] = normed.astype(BF)
            r2[l, rs, :] = r
            xb[rs, :] = y.astype(BF)
            xs[rs, :] = jnp.where(l == LAYERS - 1, cot[rs, :].astype(F32), y)
            return carry

        lax.fori_loop(0, T // ROWS, rows_of, 0)

    def save_prob(op):
        getattr(pltpu.make_async_copy(prob, P0, psem), op)()

    def compute(v, slot):
        l, k = v // PER, v % PER
        pl.when(k < 3)(lambda: do_qkv(l, k, slot))

        @pl.when((k >= 2) & (k <= 4))
        def _():
            lo = jnp.where(k == 2, 0, jnp.where(k == 3, 2, 5))
            hi = jnp.where(k == 2, 2, jnp.where(k == 3, 5, 8))
            do_attention(l, lo, hi)

        @pl.when(k == 4)
        def _():
            pl.when(l == 0)(lambda: save_prob("start"))
            do_out(l, 1 - slot)

        pl.when((k >= 4) & (k < 8))(lambda: do_inner(l, k - 4, slot))
        pl.when(k >= 8)(lambda: do_outer(l, k - 8, slot))

        @pl.when(k == PER - 1)
        def _():
            pl.when(l == 0)(lambda: save_prob("wait"))
            do_norm2(l)

    lag = (comm.stages - 1) * gap + 1

    def main(t, carry):
        v = t - lag
        slot = (v + 2 * lag) % 2
        ready = (v >= 0) & (v < UNITS)

        @pl.when(ready)
        def _():
            for core in (0, 1):

                @pl.when(c == core)
                def _():
                    comm.sibling(1 - core, v).wait_recv()

            load_unit(v, slot, "start")

        comm.tick(t)
        pl.when(t == 1)(init_x)

        @pl.when(ready)
        def _():
            load_unit(v, slot, "wait")
            compute(v, slot)

        return carry

    lax.fori_loop(0, UNITS + comm.stages * gap, main, 0)

    def results(src, out, base, op):
        mine = pl.ds(pl.multiple_of(c * half, half), half)
        theirs = pl.ds(pl.multiple_of((1 - c) * half, half), half)
        lc = pltpu.make_async_copy(src.at[mine], out.at[c], osem.at[base])
        rc = pltpu.make_async_remote_copy(
            src_ref=src.at[theirs],
            dst_ref=out.at[c],
            send_sem=osem.at[base + 1],
            recv_sem=osem.at[base + 2],
            device_id=other,
            device_id_type=MESH,
        )
        if op == "start":
            rc.start()
            lc.start()
        else:
            rc.wait_send()
            lc.wait()

    def arrived(src, out, base):
        rows = pl.ds(0, half)
        pltpu.make_async_remote_copy(
            src_ref=src.at[rows],
            dst_ref=out.at[1 - c],
            send_sem=osem.at[base + 1],
            recv_sem=osem.at[base + 2],
            device_id=other,
            device_id_type=MESH,
        ).wait_recv()

    def load(s, slot, op):
        l, k = 1 - s // PER, s % PER
        rows = (k < 8) & (k % 2 == 0)
        pl.when(rows)(lambda: load_rows(l, k // 2, slot, op))
        unit = l * PER + jnp.where(k < 8, 4 + k // 2, jnp.where(k == 8, 3, k - 9))
        pl.when(jnp.logical_not(rows))(lambda: load_unit(unit, slot, op))

    def next_weights(s):
        slot = s % 2
        load(s, slot, "wait")
        pl.when(s + 1 < UNITS)(lambda: load(s + 1, 1 - slot, "start"))
        return slot

    def norm_back(l, source, normed, r_ref, gain_ref, at_shift, at_bias, keep):
        gain = row(gain_ref, l)

        def rows_of(i, carry):
            sum_g, sum_z = carry
            rs = pl.ds(pl.multiple_of(i * ROWS, ROWS), ROWS)
            g = source[rs, :]
            nv = normed[l, rs, :].astype(F32)
            u = g * gain
            gz = r_ref[l, rs, :] * (
                u - jnp.mean(u, axis=1, keepdims=True) - nv * jnp.mean(u * nv, axis=1, keepdims=True)
            )
            keep[rs, :] = gz
            xb[rs, :] = gz.astype(BF)
            return sum_g + fold(g), sum_z + fold(gz)

        zero = jnp.zeros((8, D), F32)
        sum_g, sum_z = lax.fori_loop(0, T // ROWS, rows_of, (zero, zero))
        bg[pl.ds(l * 10 + at_shift, 1), :] = colsum(sum_g)
        bg[pl.ds(l * 10 + at_bias, 1), :] = colsum(sum_z)

    results(xb, layer_output, 0, "start")
    load(0, 0, "start")
    results(xb, layer_output, 0, "wait")

    def layer_back(i, carry):
        l = LAYERS - 1 - i
        s0 = i * PER
        norm_back(l, xs, n2, r2, second_gain, 9, 7, mid)

        def ff(f, carry):
            slot = next_weights(s0 + 2 * f)
            for i4 in range(4):
                cs = cols(f * 4 + i4)
                gh = dot(xb[...], o_rows(slot, i4), 1, 1) * gp[l, :, cs].astype(F32)
                bg[pl.ds(l * 10 + 3 + f, 1), i4 * BLK : (i4 + 1) * BLK] = colsum(fold(gh))
                act[:, cs] = gh.astype(BF)
            slot = next_weights(s0 + 2 * f + 1)
            for i4 in range(4):
                sl = slice(i4 * BLK, (i4 + 1) * BLK)
                mid[:, sl] += dot(act[:, cols(f, D)], w_rows(slot, i4), 1, 1)
            return carry

        lax.fori_loop(0, 4, ff, 0)
        norm_back(l, mid, n1, r1, first_gain, 8, 2, mid)
        slot = next_weights(s0 + 8)
        for i4 in range(4):
            sl = slice(i4 * BLK, (i4 + 1) * BLK)
            gc = dot(xb[...], w_rows(slot, i4), 1, 1).astype(BF)
            bg[pl.ds(l * 10 + 1, 1), sl] = colsum(fold(gc.astype(F32)))
            qkv[0, :, sl] = gc
            gcT[sl, :] = gc.T

        pl.when(i == 1)(lambda: load_prob("wait"))

        def pair(hp, carry):
            cs = cols(hp, 2 * HEAD)
            gc2, k2, v2 = qkv[0, :, cs], qkv[2 * l + 1, :, cs], qkv[2 * l + 2, :, cs]
            dqs = []
            for hh in (0, 1):
                hs = pl.ds(pl.multiple_of((2 * hp + hh) * HEAD, HEAD), HEAD)
                p = prob[2 * hp + hh]
                pf = p.astype(F32)
                gm = jnp.where(halves[hh], gc2 * BF(HEAD**-0.5), BF(0))
                dp = dot(gm, v2, 1, 1)
                total = jnp.sum(dp * pf, axis=1, keepdims=True)
                ds = (pf * (dp - total)).astype(BF)
                dqs.append(dot(ds, k2))
                dkT[hs, :] = dot(qT[l, hs, :], ds).astype(BF)
                dvT[hs, :] = dot(gcT[hs, :], p).astype(BF)
            dq = jnp.where(halves[0], dqs[0], dqs[1])
            dqs8[:, cs] = fold(dq)
            ctx[:, cs] = dq.astype(BF)
            return carry

        lax.fori_loop(0, HEADS // 2, pair, 0)
        bg[pl.ds(l * 10, 1), :] = colsum(dqs8[...])
        pl.when(i == 0)(lambda: load_prob("start"))

        slot = next_weights(s0 + 9)
        for i4 in range(4):
            sl = slice(i4 * BLK, (i4 + 1) * BLK)
            mid[:, sl] += dot(ctx[...], w_rows(slot, i4), 1, 1)
        slot = next_weights(s0 + 10)
        for i4 in range(4):
            sl = slice(i4 * BLK, (i4 + 1) * BLK)
            mid[:, sl] += dot(dkT[...], w_rows(slot, i4), 0, 1)
        slot = next_weights(s0 + 11)
        for i4 in range(4):
            sl = slice(i4 * BLK, (i4 + 1) * BLK)
            y = mid[:, sl] + dot(dvT[...], w_rows(slot, i4), 0, 1)
            xs[:, sl] = y
            xb[:, sl] = y.astype(BF)
        return carry

    def load_prob(op):
        getattr(pltpu.make_async_copy(P0, prob, psem), op)()

    bg[...] = jnp.zeros_like(bg)
    lax.fori_loop(0, LAYERS, layer_back, 0)
    results(xb, input_gradient, 3, "start")

    for r, to in enumerate(comm.partners()):
        cp = pltpu.make_async_remote_copy(
            src_ref=bg,
            dst_ref=arb.at[r],
            send_sem=asem.at[0, r],
            recv_sem=asem.at[1, r],
            device_id=to,
            device_id_type=MESH,
        )
        cp.start()
        cp.wait()
        bg[...] += arb[r]
    grads[...] = bg[...]
    results(xb, input_gradient, 3, "wait")
    arrived(xb, layer_output, 0)
    arrived(xb, input_gradient, 3)


def on_device(
    hidden,
    cotangent,
    lengths,
    separators,
    type_table,
    projection_weight,
    output_weight,
    inner_weight,
    outer_weight,
    query_bias,
    value_bias,
    output_bias,
    inner_bias,
    outer_bias,
    first_gain,
    first_shift,
    second_gain,
    second_shift,
):
    nb = lax.axis_size("batch")
    nz, n = sizes(nb)
    gap = 2 if nb <= 16 else 1
    stages = 1 + (n - 1) + (nz - 1) + (n - 1)
    slots = (stages + 1) * gap
    rounds = 1 + (nb.bit_length() - 1)
    T = 2 * hidden.shape[1]
    R = D // nb
    smem = pl.BlockSpec(memory_space=pltpu.SMEM)
    vmem = pl.BlockSpec(memory_space=pltpu.VMEM)
    hbm = pl.BlockSpec(memory_space=pl.ANY)
    sems = Comm.sems(nz, n)
    out_shape = (
        jax.ShapeDtypeStruct(hidden.shape, BF),
        jax.ShapeDtypeStruct(hidden.shape, BF),
        jax.ShapeDtypeStruct((24, D), F32),
        jax.ShapeDtypeStruct((UNITS, nz, n, n, R, D), BF),
        jax.ShapeDtypeStruct((HEADS, T, T), BF),
    )
    dma = pltpu.SemaphoreType.DMA
    scratch = [
        pltpu.VMEM((UNITS, R, D), BF),
        pltpu.VMEM((T, D), BF),
        pltpu.VMEM((T, D), BF),
        pltpu.VMEM((T, D), F32),
        pltpu.VMEM((T, D), BF),
        pltpu.VMEM((5, T, D), BF),
        pltpu.VMEM((LAYERS, D, T), BF),
        pltpu.VMEM((HEADS, T, T), BF),
        pltpu.VMEM((T, D), F32),
        pltpu.VMEM((T, FF), BF),
        pltpu.VMEM((LAYERS, T, FF), BF),
        pltpu.VMEM((LAYERS, T, D), BF),
        pltpu.VMEM((LAYERS, T, D), BF),
        pltpu.VMEM((LAYERS, T, 1), F32),
        pltpu.VMEM((LAYERS, T, 1), F32),
        pltpu.VMEM((D, T), BF),
        pltpu.VMEM((D, T), BF),
        pltpu.VMEM((D, T), BF),
        pltpu.VMEM((2, nz, n, n, 4, R, BLK), BF),
        pltpu.VMEM((24, D), F32),
        pltpu.VMEM((rounds, 24, D), F32),
        pltpu.VMEM((8, D), F32),
        dma((slots, sems)),
        dma((slots, sems)),
        dma((slots,)),
        dma((UNITS,)),
        dma((UNITS + 32,)),
        dma((2, 16)),
        dma((6,)),
        dma(()),
        dma((6,)),
        dma((2, rounds)),
    ]
    out = pl.pallas_call(
        functools.partial(kernel, nz, n, gap, slots),
        out_shape=out_shape,
        in_specs=[smem, smem, hbm, hbm, vmem, hbm, hbm, hbm, hbm] + [vmem] * 9,
        out_specs=(hbm, hbm, vmem, hbm, hbm),
        scratch_shapes=scratch,
        compiler_params=pltpu.CompilerParams(
            collective_id=0, has_side_effects=True, vmem_limit_bytes=60 * 2**20
        ),
        cost_estimate=pl.CostEstimate(flops=60 * 10**9, bytes_accessed=200 * 10**6, transcendentals=20 * 10**6),
    )(
        lengths,
        separators,
        hidden,
        cotangent,
        type_table,
        projection_weight,
        output_weight,
        inner_weight,
        outer_weight,
        query_bias,
        value_bias,
        output_bias,
        inner_bias,
        outer_bias,
        first_gain,
        first_shift,
        second_gain,
        second_shift,
    )
    by_layer = out[2][: LAYERS * 10].reshape(LAYERS, 10, D)
    return (
        out[0],
        out[1],
        by_layer[:, 0],
        by_layer[:, 1],
        by_layer[:, 2],
        by_layer[:, 3:7].reshape(LAYERS, FF),
        by_layer[:, 7],
        by_layer[:, 8],
        by_layer[:, 9],
    )


def solution(mesh):
    batched = P("batch", "blk", None)
    rows = P(None, "batch", None)
    return jax.shard_map(
        on_device,
        mesh=mesh,
        in_specs=(batched, batched, P("batch"), P("batch"), P(), rows, rows, rows, rows) + (P(),) * 9,
        out_specs=(batched, batched) + (P(),) * 7,
        check_vma=False,
    )
```

time: 1340 us -> 315 us (0.24)
  waiting for transfers between devices: 800 us -> 0 us
  matrix products: 337 us -> 0 us
  Pallas kernels: 0 us -> 305 us
  local copies, waits for them, and re-layouts: 99.8 us -> 7.94 us
  other arithmetic: 78.7 us -> 0 us
  between operations: 15 us -> 0.68 us
    all_gather x12 -> x0, waiting for transfers between devices: 649 us -> none  [the longest x2 217 us: on_device(): lax.all_gather(inner_weight[layer_index], 'batch', axis=0, tiled=True)]
    dot_general x44 -> x0, matrix products: 337 us -> none  [the longest x8 72.6 us: project_back(): jnp.einsum('gte,de->gtd', grad_rows, weight, preferred_element_type=jnp.f...]
    pallas_call x0 -> x1, Pallas kernels: none -> 305 us  [on_device(): pl.pallas_call(functools.partial(kernel, nz, n, gap, slots), out_shape=ou...]
    psum x1 -> x0, waiting for transfers between devices: 133 us -> none  [on_device(): lax.psum((local_terms[0], local_terms[1], local_terms[2], local_terms[3],...]
    another operation x6 -> x0, other arithmetic: 44.8 us -> none  [the longest x2 39.4 us: gelu_exact(): return jax.nn.gelu(values, approximate=False)]
    reduce_sum x20 -> x0, other arithmetic: 27.5 us -> none  [the longest x7 12.1 us: token_sum(): return jnp.sum(values, axis=(0, 1))]
    convert_element_type x10 -> x0, local copies, waits for them, and re-layouts: 23.8 us -> none  [the longest x2 8.21 us: on_device(): join_heads(key_grads).astype(jnp.bfloat16)]
    unnamed x160 -> x7, local copies, waits for them, and re-layouts: 30.4 us -> 7 us
  transfers between devices with their start and end apart: 17 -> 0, of which waited for: 15 -> 0; matrix products, arithmetic and copies ran while one was open for 15% -> 0% of each run, Pallas kernels for 0% -> 0%
where the time goes in v1:
time: 315 us; the launch traced here: 314 us
  Pallas kernels  305 us (97%)
  local copies, waits for them, and re-layouts  7.94 us (3%)
    pallas_call x1, Pallas kernels, on_device(): pl.pallas_call(functools.partial(kernel, nz, n, gap, slots), out_shape=ou...  305 us
    unnamed x7, local copies, waits for them, and re-layouts  7 us

profile of v1, /device:TPU:0, one launch (start us, length us, event | category | flops | bytes accessed | tf_op | source)
XLA Modules:
  0.0 313.9 jit_solution(15485564125399034909)
XLA Ops:
  0.7 305.3 %shard_map.241 = (bf16[2,256,1024]{2,1,0:T(8,128)(2,1)}, bf16[2,256,1024]{2,1,0:T(8,128)(2,1)}, f32[24,1024]{1,0:T(8,128)}, bf16[24,4,2,2,64,1024]{5,4,3,2,1,0:T(8,128)(2,1)}, bf16[16,512,512]{2,1,0:T(8,128)(2,1)}) custom-call(s32[2]{0:T(128)} %lengths.1, s32[2]{0:T(128)} %separators.1, bf16[2,256,1024]{2,1,0:T(8,128)(2,1)} %hidden.1, ...), custom_call_target="tpu_custom_call" | custom-call | flops 60000002048 | bytes 200000000 | tf_op jit(solution)/shard_map/pallas_call | solution.py:812
  305.9 0.9 reshape.24
  306.9 0.6 copy.39
  307.6 0.6 copy_bitcast_fusion
  308.2 0.6 copy_bitcast_fusion.2
  308.8 0.6 copy_bitcast_fusion.4
  309.4 2.3 copy.48
  311.6 2.3 copy.49
  (2 shorter events, 0.0 us)

commit v2 on v1

--- a/solution.py
+++ b/solution.py
@@ -191,12 +191,14 @@
             device_id_type=MESH,
         )
 
-    def tick(self, t):
+    def tick(self, t, part):
+        order = [self.stages, *reversed(range(self.stages))]
+        cut = len(order) // 2
         for core in (0, 1):
 
             @pl.when(self.c == core)
             def _():
-                for k in [self.stages, *reversed(range(self.stages))]:
+                for k in order[:cut] if part == 0 else order[cut:]:
                     u = t - k * self.gap
                     for par in (0, 1):
 
@@ -207,31 +209,82 @@
                             else:
                                 self.run(core, par, u, k, "start")
 
-    def partners(self):
-        yield (self.b, 1 - self.c)
-        step = 1
-        while step < self.nz * self.n * self.n:
-            yield (self.b + step * (1 - 2 * ((self.b // step) % 2)), self.c)
-            step *= 2
-
     def barrier(self):
         bar = pltpu.get_barrier_semaphore()
-        n, nz = self.n, self.nz
-        total = jnp.int32(0)
-        for to in self.partners():
-            pl.semaphore_signal(bar, inc=1, device_id=to, device_id_type=MESH)
-            total = total + 1
-        for length, pos, stride in ((n, self.x, 1), (n, self.y, n), (nz, self.z, n * n)):
-            for d in (0, 1):
-                ok = (pos + 1 < length) if d == 0 else (pos >= 1)
-                total = total + ok.astype(jnp.int32)
-
-                @pl.when(ok)
-                def _():
-                    to = (self.b + (stride if d == 0 else -stride), self.c)
-                    pl.semaphore_signal(bar, inc=1, device_id=to, device_id_type=MESH)
-
-        pl.semaphore_wait(bar, total)
+        plane, me = 2 * self.n * self.n, self.place()
+
+        def in_plane(i, carry):
+            to = (me + i) % plane
+            pl.semaphore_signal(bar, inc=1, device_id=self.at(to), device_id_type=MESH)
+            return carry
+
+        def along_z(i, carry):
+            pl.semaphore_signal(bar, inc=1, device_id=self.along((self.z + i) % self.nz), device_id_type=MESH)
+            return carry
+
+        lax.fori_loop(1, plane, in_plane, 0)
+        lax.fori_loop(1, self.nz, along_z, 0)
+        pl.semaphore_wait(bar, plane - 1 + self.nz - 1)
+
+    def place(self):
+        return (self.b % (self.n * self.n)) * 2 + self.c
+
+    def at(self, p):
+        return (self.z * self.n * self.n + p // 2, p % 2)
+
+    def along(self, z):
+        return (z * self.n * self.n + self.b % (self.n * self.n), self.c)
+
+
+class Total:
+    def __init__(self, comm, phase, l, lo, hi, bg, planes, part, lines, total, sems):
+        self.comm, self.phase, self.l, self.rows = comm, phase, l, pl.ds(lo, hi - lo)
+        self.bg, self.planes, self.part, self.lines, self.total = bg, planes, part, lines, total
+        self.sems = sems
+
+    def copies(self, second, op):
+        comm, l, rows = self.comm, self.l, self.rows
+        me, count = (comm.z, comm.nz) if second else (comm.place(), 2 * comm.n * comm.n)
+        src, dst = (self.part, self.lines) if second else (self.bg, self.planes)
+
+        def one(i, carry):
+            peer = (me + i) % count
+            to = comm.along(peer) if second else comm.at(peer)
+            slot = peer if op == "wait_recv" else me
+            cp = pltpu.make_async_remote_copy(
+                src_ref=src.at[l, rows],
+                dst_ref=dst.at[l, slot, rows],
+                send_sem=self.sems[2 * second].at[self.phase, i],
+                recv_sem=self.sems[2 * second + 1].at[self.phase, slot],
+                device_id=to,
+                device_id_type=MESH,
+            )
+            getattr(cp, op)()
+            return carry
+
+        lax.fori_loop(1, count, one, 0)
+
+    def add(self, second):
+        me, count = (self.comm.z, self.comm.nz) if second else (self.comm.place(), 2 * self.comm.n * self.comm.n)
+        src, buf, dst = (self.part, self.lines, self.total) if second else (self.bg, self.planes, self.part)
+        self.copies(second, "wait_recv")
+        buf[self.l, me, self.rows] = src[self.l, self.rows]
+
+        def one(i, acc):
+            return acc + buf[self.l, i, self.rows]
+
+        dst[self.l, self.rows] = lax.fori_loop(1, count, one, buf[self.l, 0, self.rows])
+        self.copies(second, "wait_send")
+
+    def start(self):
+        self.copies(0, "start")
+
+    def middle(self):
+        self.add(0)
+        self.copies(1, "start")
+
+    def finish(self):
+        self.add(1)
 
 
 def dot(a, b, ca=1, cb=0):
@@ -272,7 +325,7 @@
     second_shift,
     layer_output,
     input_gradient,
-    grads,
+    total,
     G,
     P0,
     stg,
@@ -295,7 +348,9 @@
     dvT,
     wbuf,
     bg,
-    arb,
+    planes,
+    part,
+    lines,
     dqs8,
     ssem,
     rsem,
@@ -306,7 +361,7 @@
     xsem,
     psem,
     osem,
-    asem,
+    *asems,
 ):
     nb = nz * n * n
     R = D // nb
@@ -445,10 +500,11 @@
         normed = centred * r
         return normed, r, normed * gain + shift
 
-    def do_qkv(l, j, slot):
+    def do_qkv(l, j, slot, lo, hi):
         is_q, is_v = (j == 0).astype(F32), (j == 2).astype(F32)
         at = jnp.where(j == 0, 0, 2 * l + j)
-        for g in range(4):
+
+        for g in range(lo, hi):
             sl = slice(g * BLK, (g + 1) * BLK)
             bias = query_bias[pl.ds(l, 1), sl] * is_q + value_bias[pl.ds(l, 1), sl] * is_v
             qkv[at, :, sl] = (dot(xb[...], w_cols(slot, g)) + bias).astype(BF)
@@ -490,18 +546,22 @@
 
         lax.fori_loop(0, T // ROWS, rows_of, 0)
 
-    def do_inner(l, i, slot):
-        for g in range(4):
-            cs = cols(i * 4 + g)
-            h = dot(xb[...], w_cols(slot, g)) + inner_bias[pl.ds(l, 1), cs]
+    def do_inner(l, lo, hi):
+        def block(i, carry):
+            cs = cols(i)
+            h = dot(xb[...], w_cols((l * PER + 4 + i // 4) % 3, i % 4)) + inner_bias[pl.ds(l, 1), cs]
             cdf = 0.5 + 0.5 * lax.erf(h * (0.5**0.5))
             act[:, cs] = (h * cdf).astype(BF)
             gp[l, :, cs] = (cdf + h * (jnp.exp(-0.5 * h * h) * 0.3989422804014327)).astype(BF)
-
-    def do_outer(l, j, slot):
+            return carry
+
+        lax.fori_loop(lo, hi, block, 0)
+
+    def do_outer(l, j, slot, part):
         cs = cols(j)
+        rs = slice(part * half, (part + 1) * half)
         w = wbuf[slot].reshape(FF, BLK)
-        xs[:, cs] = mid[:, cs] + dot(act[...], w) + outer_bias[pl.ds(l, 1), cs]
+        xs[rs, cs] = mid[rs, cs] + dot(act[rs, :], w) + outer_bias[pl.ds(l, 1), cs]
 
     def do_norm2(l):
         gain, shift = row(second_gain, l), row(second_shift, l)
@@ -520,34 +580,44 @@
     def save_prob(op):
         getattr(pltpu.make_async_copy(prob, P0, psem), op)()
 
-    def compute(v, slot):
+    def compute(v, slot, part):
         l, k = v // PER, v % PER
-        pl.when(k < 3)(lambda: do_qkv(l, k, slot))
+        pl.when(k < 3)(lambda: do_qkv(l, k, slot, 2 * part, 2 * part + 2))
 
         @pl.when((k >= 2) & (k <= 4))
         def _():
-            lo = jnp.where(k == 2, 0, jnp.where(k == 3, 2, 5))
-            hi = jnp.where(k == 2, 2, jnp.where(k == 3, 5, 8))
-            do_attention(l, lo, hi)
-
-        @pl.when(k == 4)
+            if part == 0:
+                do_attention(l, jnp.where(k == 2, 0, jnp.where(k == 3, 1, 5)), jnp.where(k == 2, 0, jnp.where(k == 3, 3, 8)))
+            else:
+                do_attention(l, jnp.where(k == 2, 0, 3), jnp.where(k == 2, 1, jnp.where(k == 3, 5, 3)))
+
+        if part == 1:
+
+            @pl.when(k == 4)
+            def _():
+                pl.when(l == 0)(lambda: save_prob("start"))
+                do_out(l, (v + 2) % 3)
+
+        @pl.when((k >= 5) & (k < 8))
         def _():
-            pl.when(l == 0)(lambda: save_prob("start"))
-            do_out(l, 1 - slot)
-
-        pl.when((k >= 4) & (k < 8))(lambda: do_inner(l, k - 4, slot))
-        pl.when(k >= 8)(lambda: do_outer(l, k - 8, slot))
-
-        @pl.when(k == PER - 1)
-        def _():
-            pl.when(l == 0)(lambda: save_prob("wait"))
-            do_norm2(l)
+            if part == 0:
+                do_inner(l, jnp.where(k == 5, 0, 4 * (k - 4)), jnp.where(k == 5, 4, 4 * (k - 4) + 2))
+            else:
+                do_inner(l, jnp.where(k == 5, 4, 4 * (k - 4) + 2), 4 * (k - 4) + 4)
+
+        pl.when(k >= 8)(lambda: do_outer(l, k - 8, slot, part))
+        if part == 1:
+
+            @pl.when(k == PER - 1)
+            def _():
+                pl.when(l == 0)(lambda: save_prob("wait"))
+                do_norm2(l)
 
     lag = (comm.stages - 1) * gap + 1
 
     def main(t, carry):
         v = t - lag
-        slot = (v + 2 * lag) % 2
+        slot = (v + 3 * lag) % 3
         ready = (v >= 0) & (v < UNITS)
 
         @pl.when(ready)
@@ -560,13 +630,16 @@
 
             load_unit(v, slot, "start")
 
-        comm.tick(t)
+        comm.tick(t, 0)
         pl.when(t == 1)(init_x)
 
         @pl.when(ready)
         def _():
             load_unit(v, slot, "wait")
-            compute(v, slot)
+            compute(v, slot, 0)
+
+        comm.tick(t, 1)
+        pl.when(ready)(lambda: compute(v, slot, 1))
 
         return carry
 
@@ -610,10 +683,13 @@
         pl.when(jnp.logical_not(rows))(lambda: load_unit(unit, slot, op))
 
     def next_weights(s):
-        slot = s % 2
-        load(s, slot, "wait")
-        pl.when(s + 1 < UNITS)(lambda: load(s + 1, 1 - slot, "start"))
-        return slot
+        load(s, s % 3, "wait")
+        pl.when(s + 2 < UNITS)(lambda: load(s + 2, (s + 2) % 3, "start"))
+        return s % 3
+
+    def keep_sum(l, k, values):
+        for i in range(values.shape[1] // 128):
+            bg[l, k, i : i + 1, :] = values[:, i * 128 : (i + 1) * 128]
 
     def norm_back(l, source, normed, r_ref, gain_ref, at_shift, at_bias, keep):
         gain = row(gain_ref, l)
@@ -633,24 +709,28 @@
 
         zero = jnp.zeros((8, D), F32)
         sum_g, sum_z = lax.fori_loop(0, T // ROWS, rows_of, (zero, zero))
-        bg[pl.ds(l * 10 + at_shift, 1), :] = colsum(sum_g)
-        bg[pl.ds(l * 10 + at_bias, 1), :] = colsum(sum_z)
+        keep_sum(l, at_shift, colsum(sum_g))
+        keep_sum(l, at_bias, colsum(sum_z))
 
     results(xb, layer_output, 0, "start")
     load(0, 0, "start")
+    load(1, 1, "start")
     results(xb, layer_output, 0, "wait")
 
     def layer_back(i, carry):
         l = LAYERS - 1 - i
         s0 = i * PER
-        norm_back(l, xs, n2, r2, second_gain, 9, 7, mid)
+        norm_back(l, xs, n2, r2, second_gain, 8, 6, mid)
+        pl.when(i == 1)(totals[0].start)
 
         def ff(f, carry):
             slot = next_weights(s0 + 2 * f)
             for i4 in range(4):
                 cs = cols(f * 4 + i4)
                 gh = dot(xb[...], o_rows(slot, i4), 1, 1) * gp[l, :, cs].astype(F32)
-                bg[pl.ds(l * 10 + 3 + f, 1), i4 * BLK : (i4 + 1) * BLK] = colsum(fold(gh))
+                sums = colsum(fold(gh))
+                bg[l, 2 + f, 2 * i4 : 2 * i4 + 1, :] = sums[:, :128]
+                bg[l, 2 + f, 2 * i4 + 1 : 2 * i4 + 2, :] = sums[:, 128:]
                 act[:, cs] = gh.astype(BF)
             slot = next_weights(s0 + 2 * f + 1)
             for i4 in range(4):
@@ -659,16 +739,23 @@
             return carry
 
         lax.fori_loop(0, 4, ff, 0)
-        norm_back(l, mid, n1, r1, first_gain, 8, 2, mid)
+        pl.when(i == 1)(totals[0].middle)
+        norm_back(l, mid, n1, r1, first_gain, 7, 1, mid)
         slot = next_weights(s0 + 8)
         for i4 in range(4):
             sl = slice(i4 * BLK, (i4 + 1) * BLK)
             gc = dot(xb[...], w_rows(slot, i4), 1, 1).astype(BF)
-            bg[pl.ds(l * 10 + 1, 1), sl] = colsum(fold(gc.astype(F32)))
+            sums = colsum(fold(gc.astype(F32)))
+            bg[l, 0, 2 * i4 : 2 * i4 + 1, :] = sums[:, :128]
+            bg[l, 0, 2 * i4 + 1 : 2 * i4 + 2, :] = sums[:, 128:]
             qkv[0, :, sl] = gc
             gcT[sl, :] = gc.T
 
-        pl.when(i == 1)(lambda: load_prob("wait"))
+        @pl.when(i == 1)
+        def _():
+            load_prob("wait")
+            totals[0].finish()
+            totals[1].start()
 
         def pair(hp, carry):
             cs = cols(hp, 2 * HEAD)
@@ -691,8 +778,17 @@
             return carry
 
         lax.fori_loop(0, HEADS // 2, pair, 0)
-        bg[pl.ds(l * 10, 1), :] = colsum(dqs8[...])
-        pl.when(i == 0)(lambda: load_prob("start"))
+        keep_sum(l, 9, colsum(dqs8[...]))
+
+        @pl.when(i == 0)
+        def _():
+            load_prob("start")
+
+        @pl.when(i == 1)
+        def _():
+            totals[2].start()
+            totals[1].middle()
+
 
         slot = next_weights(s0 + 9)
         for i4 in range(4):
@@ -702,6 +798,7 @@
         for i4 in range(4):
             sl = slice(i4 * BLK, (i4 + 1) * BLK)
             mid[:, sl] += dot(dkT[...], w_rows(slot, i4), 0, 1)
+        pl.when(i == 1)(totals[2].middle)
         slot = next_weights(s0 + 11)
         for i4 in range(4):
             sl = slice(i4 * BLK, (i4 + 1) * BLK)
@@ -713,26 +810,55 @@
     def load_prob(op):
         getattr(pltpu.make_async_copy(P0, prob, psem), op)()
 
-    bg[...] = jnp.zeros_like(bg)
+    totals = [
+        Total(comm, phase, l, lo, hi, bg, planes, part, lines, total, asems)
+        for phase, (l, lo, hi) in enumerate(((1, 0, 10), (0, 0, 9), (0, 9, 10)))
+    ]
     lax.fori_loop(0, LAYERS, layer_back, 0)
     results(xb, input_gradient, 3, "start")
-
-    for r, to in enumerate(comm.partners()):
-        cp = pltpu.make_async_remote_copy(
-            src_ref=bg,
-            dst_ref=arb.at[r],
-            send_sem=asem.at[0, r],
-            recv_sem=asem.at[1, r],
-            device_id=to,
-            device_id_type=MESH,
-        )
-        cp.start()
-        cp.wait()
-        bg[...] += arb[r]
-    grads[...] = bg[...]
+    totals[1].finish()
+    totals[2].finish()
     results(xb, input_gradient, 3, "wait")
     arrived(xb, layer_output, 0)
     arrived(xb, input_gradient, 3)
+
+
+def finish(first, second, total, *rest):
+    outs, (buf, into, outof) = rest[:9], rest[9:]
+    half = first.shape[1] // 2
+    moves = []
+    for i, (src, dst) in enumerate(((first, outs[0]), (second, outs[1]))):
+        for j in range(2):
+            rows = pl.ds(j * half, half)
+            k = 2 * i + j
+            moves.append(
+                (
+                    pltpu.make_async_copy(src.at[:, rows], buf.at[k], into.at[k]),
+                    pltpu.make_async_copy(buf.at[k], dst.at[:, rows], outof.at[k]),
+                )
+            )
+    for here, _ in moves:
+        here.start()
+    for l in range(LAYERS):
+        for k, out, at in (
+            (9, outs[2], 0),
+            (0, outs[3], 0),
+            (1, outs[4], 0),
+            (2, outs[5], 0),
+            (3, outs[5], 1),
+            (4, outs[5], 2),
+            (5, outs[5], 3),
+            (6, outs[6], 0),
+            (7, outs[7], 0),
+            (8, outs[8], 0),
+        ):
+            for i in range(8):
+                out[l : l + 1, at * D + i * 128 : at * D + (i + 1) * 128] = total[l, k, i : i + 1, :]
+    for here, there in moves:
+        here.wait()
+        there.start()
+    for _, there in moves:
+        there.wait()
 
 
 def on_device(
@@ -760,7 +886,7 @@
     gap = 2 if nb <= 16 else 1
     stages = 1 + (n - 1) + (nz - 1) + (n - 1)
     slots = (stages + 1) * gap
-    rounds = 1 + (nb.bit_length() - 1)
+    plane = 2 * n * n
     T = 2 * hidden.shape[1]
     R = D // nb
     smem = pl.BlockSpec(memory_space=pltpu.SMEM)
@@ -770,7 +896,7 @@
     out_shape = (
         jax.ShapeDtypeStruct(hidden.shape, BF),
         jax.ShapeDtypeStruct(hidden.shape, BF),
-        jax.ShapeDtypeStruct((24, D), F32),
+        jax.ShapeDtypeStruct((LAYERS, 10, 8, 128), F32),
         jax.ShapeDtypeStruct((UNITS, nz, n, n, R, D), BF),
         jax.ShapeDtypeStruct((HEADS, T, T), BF),
     )
@@ -794,20 +920,25 @@
         pltpu.VMEM((D, T), BF),
         pltpu.VMEM((D, T), BF),
         pltpu.VMEM((D, T), BF),
-        pltpu.VMEM((2, nz, n, n, 4, R, BLK), BF),
-        pltpu.VMEM((24, D), F32),
-        pltpu.VMEM((rounds, 24, D), F32),
+        pltpu.VMEM((3, nz, n, n, 4, R, BLK), BF),
+        pltpu.VMEM((LAYERS, 10, 8, 128), F32),
+        pltpu.VMEM((LAYERS, plane, 10, 8, 128), F32),
+        pltpu.VMEM((LAYERS, 10, 8, 128), F32),
+        pltpu.VMEM((LAYERS, nz, 10, 8, 128), F32),
         pltpu.VMEM((8, D), F32),
         dma((slots, sems)),
         dma((slots, sems)),
         dma((slots,)),
         dma((UNITS,)),
         dma((UNITS + 32,)),
-        dma((2, 16)),
+        dma((3, 16)),
         dma((6,)),
         dma(()),
         dma((6,)),
-        dma((2, rounds)),
+        dma((3, plane)),
+        dma((3, plane)),
+        dma((3, nz)),
+        dma((3, nz)),
     ]
     out = pl.pallas_call(
         functools.partial(kernel, nz, n, gap, slots),
@@ -839,17 +970,21 @@
         second_gain,
         second_shift,
     )
-    by_layer = out[2][: LAYERS * 10].reshape(LAYERS, 10, D)
-    return (
-        out[0],
-        out[1],
-        by_layer[:, 0],
-        by_layer[:, 1],
-        by_layer[:, 2],
-        by_layer[:, 3:7].reshape(LAYERS, FF),
-        by_layer[:, 7],
-        by_layer[:, 8],
-        by_layer[:, 9],
+    half = hidden.shape[1] // 2
+    return tuple(
+        pl.pallas_call(
+            finish,
+            out_shape=(
+                jax.ShapeDtypeStruct(hidden.shape, BF),
+                jax.ShapeDtypeStruct(hidden.shape, BF),
+                *(jax.ShapeDtypeStruct(b.shape, F32) for b in (
+                    query_bias, value_bias, output_bias, inner_bias, outer_bias, first_shift, second_shift
+                )),
+            ),
+            in_specs=[hbm, hbm, vmem],
+            out_specs=(hbm, hbm) + (vmem,) * 7,
+            scratch_shapes=[pltpu.VMEM((4, 2, half, D), BF), dma((4,)), dma((4,))],
+        )(out[0], out[1], out[2])
     )
 
 

time: 315 us -> 302 us (0.959)
  local copies, waits for them, and re-layouts: 7.94 us -> 0 us
  Pallas kernels: 305 us -> 300 us
    pallas_call x1, Pallas kernels: 305 us -> 296 us  [on_device(): pl.pallas_call(functools.partial(kernel, nz, n, gap, slots), out_shape=ou...]
    unnamed x7 -> x0, local copies, waits for them, and re-layouts: 7 us -> none
    pallas_call x0 -> x1, Pallas kernels: none -> 3.94 us  [on_device(): pl.pallas_call(finish, out_shape=(jax.ShapeDtypeStruct(hidden.shape, BF),...]
where the time goes in v2:
time: 302 us; the launch traced here: 301 us
  Pallas kernels  300 us (99%)
    pallas_call x1, Pallas kernels, on_device(): pl.pallas_call(functools.partial(kernel, nz, n, gap, slots), out_shape=ou...  296 us

profile of v2, /device:TPU:0, one launch (start us, length us, event | category | flops | bytes accessed | tf_op | source)
XLA Modules:
  0.0 301.0 jit_solution(17778430464478759676)
XLA Ops:
  0.6 296.3 %shard_map.241 = (bf16[2,256,1024]{2,1,0:T(8,128)(2,1)}, bf16[2,256,1024]{2,1,0:T(8,128)(2,1)}, f32[2,10,8,128]{3,2,1,0:T(8,128)}, bf16[24,4,2,2,64,1024]{5,4,3,2,1,0:T(8,128)(2,1)}, bf16[16,512,512]{2,1,0:T(8,128)(2,1)}) custom-call(s32[2]{0:T(128)} %lengths.1, s32[2]{0:T(128)} %separators.1, bf16[2,256,1024]{2,1,0:T(8,128)(2,1)} %hidden.1, ...), custom_call_target="tpu_custom_call" | custom-call | flops 60000002048 | bytes 200000000 | tf_op jit(solution)/shard_map/pallas_call | solution.py:943
  296.9 3.9 %shard_map.242 = (bf16[2,256,1024]{2,1,0:T(8,128)(2,1)}, bf16[2,256,1024]{2,1,0:T(8,128)(2,1)}, f32[2,1024]{1,0:T(2,128)}, f32[2,1024]{1,0:T(2,128)}, f32[2,1024...) custom-call(bf16[2,256,1024]{2,1,0:T(8,128)(2,1)} %get-tuple-element.12.first, ...), custom_call_target="tpu_custom_call" | custom-call | tf_op jit(solution)/shard_map/pallas_call | solution.py:975

commit v3 on v2

--- a/solution.py
+++ b/solution.py
@@ -34,19 +34,19 @@
 
 
 class Comm:
-    def __init__(self, nz, n, gathered, ssem, rsem, sib_s, sib_r, slots, gap):
-        self.nz, self.n, self.G = nz, n, gathered
+    def __init__(self, nz, n, gathered, stg, ssem, rsem, sib_s, sib_r, slots, gap):
+        self.nz, self.n, self.G, self.stg = nz, n, gathered, stg
         self.ssem, self.rsem, self.sib_s, self.sib_r = ssem, rsem, sib_s, sib_r
         self.slots, self.gap = slots, gap
         self.b = lax.axis_index("batch")
         self.c = lax.axis_index("blk")
         self.z, self.y, self.x = self.b // (n * n), (self.b // n) % n, self.b % n
         self.stages = 1 + (n - 1) + (nz - 1) + (n - 1)
-        self.fbase = 2 * (nz - 1)
+        self.fbase = nz
 
     @staticmethod
     def sems(nz, n):
-        return 2 * (nz - 1) + 2 * nz * lane(n)
+        return 2 * nz + 1 if n == 2 else nz + 2 * nz * lane(n)
 
     def cols(self, core):
         return pl.ds(0, SPLIT) if core == 0 else pl.ds(SPLIT, D - SPLIT)
@@ -66,7 +66,7 @@
         return pltpu.make_async_remote_copy(
             src_ref=ref,
             dst_ref=ref,
-            send_sem=self.ssem.at[self.slot, idx],
+            send_sem=self.ssem.at[self.slot],
             recv_sem=self.rsem.at[self.slot, idx],
             device_id=(to, self.c),
             device_id_type=MESH,
@@ -81,12 +81,12 @@
         else:
             cp.wait_send()
 
-    def arrive(self, ref, base, pos, length, stride, j, e, mode):
+    def arrive(self, ref, base, pos, length, stride, j, e, mode, last=False):
         if length == 2:
             to = self.b + stride * (1 - 2 * pos)
             if j == 0:
                 self.act(self.copy(ref(pos), base, to), mode)
-            elif mode == "start":
+            elif mode == "start" and not last:
                 self.copy(ref(1 - pos), base, to).wait_recv()
             return
         if j == 0:
@@ -140,13 +140,13 @@
             def along_z():
                 ref = self.sl(zi, fi, s)
                 if h and mode == "start":
-                    self.copy(ref, 2 * (h - 1) + d, b).wait_recv()
+                    self.copy(ref, zi, b).wait_recv()
                 if h < nz - 1:
                     for dd in (0, 1) if h == 0 else (d,):
 
                         @pl.when((z + 1 < nz) if dd == 0 else (z >= 1))
                         def _():
-                            self.act(self.copy(ref, 2 * h + dd, b + (n * n if dd == 0 else -n * n)), mode)
+                            self.act(self.copy(ref, zi, b + (n * n if dd == 0 else -n * n)), mode)
 
             def in_plane(step):
                 q = step
@@ -159,9 +159,8 @@
                     q = step - (n - 1)
                 if q >= 0:
                     for e in self.dirs(n) if q else (0,):
-                        self.arrive(
-                            lambda i: self.sl(zi, slice(None), i), sbase + zi * lw, s, n, self.sstr, q, e, mode
-                        )
+                        at = sbase if n == 2 else sbase + zi * lw
+                        self.arrive(lambda i: self.sl(zi, slice(None), i), at, s, n, self.sstr, q, e, mode, True)
 
             def events():
                 for step in range(last + 1):
@@ -176,9 +175,33 @@
                 else:
                     pl.when((zi >= 0) if d == 0 else (zi < nz))(events)
         if k == self.stages - 1:
+            if n == 2:
+                self.copy(self.sl(slice(None), slice(None), 1 - s), sbase, b).wait_recv()
             self.sibling(core, u).start()
-        if k is None:
-            self.sibling(core, u).wait_send()
+
+    def drain(self, core, par, u):
+        n, nz = self.n, self.nz
+        if n == 2:
+            slot, cs = u % self.slots, self.cols(core)
+            for z in range(nz):
+                along = (z + 1 if z < nz - 1 else 0) + (nz - z if z else 0)
+                pieces = 1 + 2 * along + 2 * nz if core == 0 else along + 3 * nz
+                same = self.stg.at[0:pieces, :, cs]
+
+                @pl.when(self.z == z)
+                def _():
+                    pltpu.make_async_remote_copy(
+                        src_ref=same,
+                        dst_ref=same,
+                        send_sem=self.ssem.at[slot],
+                        recv_sem=self.rsem.at[slot, 0],
+                        device_id=(self.b, 1 - self.c),
+                        device_id_type=MESH,
+                    ).wait_send()
+
+        else:
+            self.run(core, par, u, None, "drain")
+        self.sibling(core, u).wait_send()
 
     def sibling(self, core, u):
         ref = self.G.at[u, :, :, :, :, self.cols(core)]
@@ -186,7 +209,7 @@
             src_ref=ref,
             dst_ref=ref,
             send_sem=self.sib_s.at[u % self.slots],
-            recv_sem=self.sib_r.at[u],
+            recv_sem=self.sib_r.at[u % self.slots],
             device_id=(self.b, 1 - self.c),
             device_id_type=MESH,
         )
@@ -205,7 +228,7 @@
                         @pl.when((u >= 0) & (u < UNITS) & (u % 2 == par))
                         def _():
                             if k == self.stages:
-                                self.run(core, par, u, None, "drain")
+                                self.drain(core, par, u)
                             else:
                                 self.run(core, par, u, k, "start")
 
@@ -242,46 +265,56 @@
         self.bg, self.planes, self.part, self.lines, self.total = bg, planes, part, lines, total
         self.sems = sems
 
-    def copies(self, second, op):
+    def ends(self, second):
+        if second:
+            return self.part, self.lines, self.comm.z, self.comm.nz
+        return self.bg, self.planes, self.comm.place(), 2 * self.comm.n * self.comm.n
+
+    def copy(self, second, src, dst, to):
+        return pltpu.make_async_remote_copy(
+            src_ref=src,
+            dst_ref=dst,
+            send_sem=self.sems.at[self.phase, 2 * second],
+            recv_sem=self.sems.at[self.phase, 2 * second + 1],
+            device_id=to,
+            device_id_type=MESH,
+        )
+
+    def send(self, second):
         comm, l, rows = self.comm, self.l, self.rows
-        me, count = (comm.z, comm.nz) if second else (comm.place(), 2 * comm.n * comm.n)
-        src, dst = (self.part, self.lines) if second else (self.bg, self.planes)
+        src, dst, me, count = self.ends(second)
 
         def one(i, carry):
             peer = (me + i) % count
             to = comm.along(peer) if second else comm.at(peer)
-            slot = peer if op == "wait_recv" else me
-            cp = pltpu.make_async_remote_copy(
-                src_ref=src.at[l, rows],
-                dst_ref=dst.at[l, slot, rows],
-                send_sem=self.sems[2 * second].at[self.phase, i],
-                recv_sem=self.sems[2 * second + 1].at[self.phase, slot],
-                device_id=to,
-                device_id_type=MESH,
-            )
-            getattr(cp, op)()
+            self.copy(second, src.at[l, rows], dst.at[l, me, rows], to).start()
             return carry
 
         lax.fori_loop(1, count, one, 0)
 
+    def every(self, second):
+        _, dst, _, count = self.ends(second)
+        all_of = dst.at[self.l, pl.ds(0, count - 1), self.rows]
+        return self.copy(second, all_of, all_of, (self.comm.b, 1 - self.comm.c))
+
     def add(self, second):
-        me, count = (self.comm.z, self.comm.nz) if second else (self.comm.place(), 2 * self.comm.n * self.comm.n)
-        src, buf, dst = (self.part, self.lines, self.total) if second else (self.bg, self.planes, self.part)
-        self.copies(second, "wait_recv")
+        src, buf, me, count = self.ends(second)
+        out = self.total if second else self.part
+        self.every(second).wait_recv()
         buf[self.l, me, self.rows] = src[self.l, self.rows]
 
         def one(i, acc):
             return acc + buf[self.l, i, self.rows]
 
-        dst[self.l, self.rows] = lax.fori_loop(1, count, one, buf[self.l, 0, self.rows])
-        self.copies(second, "wait_send")
+        out[self.l, self.rows] = lax.fori_loop(1, count, one, buf[self.l, 0, self.rows])
+        self.every(second).wait_send()
 
     def start(self):
-        self.copies(0, "start")
+        self.send(0)
 
     def middle(self):
         self.add(0)
-        self.copies(1, "start")
+        self.send(1)
 
     def finish(self):
         self.add(1)
@@ -309,11 +342,26 @@
     separators,
     hidden,
     cotangent,
-    type_table,
+    type_table_in,
     proj,
     outw,
     inner,
     outer,
+    query_bias_in,
+    value_bias_in,
+    output_bias_in,
+    inner_bias_in,
+    outer_bias_in,
+    first_gain_in,
+    first_shift_in,
+    second_gain_in,
+    second_shift_in,
+    layer_output,
+    input_gradient,
+    total,
+    G,
+    P0,
+    type_table,
     query_bias,
     value_bias,
     output_bias,
@@ -323,11 +371,6 @@
     first_shift,
     second_gain,
     second_shift,
-    layer_output,
-    input_gradient,
-    total,
-    G,
-    P0,
     stg,
     xin,
     cot,
@@ -360,48 +403,44 @@
     wsem,
     xsem,
     psem,
+    vsem,
     osem,
-    *asems,
+    asems,
 ):
     nb = nz * n * n
     R = D // nb
     T = xs.shape[0]
     half = T // 2
     quarter = nb // 4
-    comm = Comm(nz, n, G, ssem, rsem, sib_s, sib_r, slots, gap)
+    comm = Comm(nz, n, G, stg, ssem, rsem, sib_s, sib_r, slots, gap)
     c = comm.c
     other = (comm.b, 1 - c)
     ctx = xin
 
-    def stage_in(op):
+    def stage_in():
         for l in range(LAYERS):
             for u in range(8):
                 m, j = (proj, u) if u < 3 else (outw, 0) if u == 3 else (inner, u - 4)
-                cp = pltpu.make_async_copy(m.at[l, :, pl.ds(j * D, D)], stg.at[l * PER + u], lsem.at[l * PER + u])
-                getattr(cp, op)()
+                pltpu.make_async_copy(m.at[l, :, pl.ds(j * D, D)], stg.at[l * PER + u], lsem.at[0]).start()
             for j in range(4):
                 for g in range(4):
-                    cp = pltpu.make_async_copy(
+                    pltpu.make_async_copy(
                         outer.at[l, pl.ds(g * R, R), pl.ds(j * BLK, BLK)],
                         stg.at[l * PER + 8 + j, :, pl.ds(g * BLK, BLK)],
-                        lsem.at[UNITS + (l * 4 + j) * 4 + g],
-                    )
-                    getattr(cp, op)()
-
-    def place(op):
+                        lsem.at[0],
+                    ).start()
+
+    def place():
+        pltpu.make_async_copy(stg, stg, lsem.at[0]).wait()
         for core in (0, 1):
 
             @pl.when(c == core)
             def _():
-                def one(u, carry):
-                    cs = comm.cols(core)
-                    cp = pltpu.make_async_copy(
-                        stg.at[u, :, cs], G.at[u, comm.z, comm.y, comm.x, :, cs], lsem.at[u]
-                    )
-                    getattr(cp, op)()
-                    return carry
-
-                lax.fori_loop(0, UNITS, one, 0)
+                cs = comm.cols(core)
+                to = G.at[:, comm.z, comm.y, comm.x, :, cs]
+                cp = pltpu.make_async_copy(stg.at[:, :, cs], to, lsem.at[1])
+                cp.start()
+                cp.wait()
 
     def exchange(op):
         for i, (src, dst) in enumerate(((hidden, xin), (cotangent, cot))):
@@ -418,12 +457,28 @@
             getattr(lc, op)()
             getattr(rc, op)()
 
-    stage_in("start")
+    vectors = (
+        (type_table_in, type_table),
+        (query_bias_in, query_bias),
+        (value_bias_in, value_bias),
+        (output_bias_in, output_bias),
+        (inner_bias_in, inner_bias),
+        (outer_bias_in, outer_bias),
+        (first_gain_in, first_gain),
+        (first_shift_in, first_shift),
+        (second_gain_in, second_gain),
+        (second_shift_in, second_shift),
+    )
+
+    def small(op):
+        for i, (src, dst) in enumerate(vectors):
+            getattr(pltpu.make_async_copy(src, dst, vsem.at[i]), op)()
+
+    stage_in()
+    small("start")
     comm.barrier()
     exchange("start")
-    stage_in("wait")
-    place("start")
-    place("wait")
+    place()
 
     def row(ref, l):
         return ref[pl.ds(l, 1), :]
@@ -436,6 +491,7 @@
 
     def init_x():
         exchange("wait")
+        small("wait")
         t0 = type_table[0:1, :].astype(F32)
         t1 = type_table[1:2, :].astype(F32)
         sep = separators[c]
@@ -451,47 +507,39 @@
 
         lax.fori_loop(0, T // ROWS, rows_of, 0)
 
-    def load_unit(u, slot, op):
-        def one(g, carry):
-            cp = pltpu.make_async_copy(
-                G.at[u, :, :, :, :, cols(g)], wbuf.at[slot, :, :, :, g], wsem.at[slot, g]
-            )
-            getattr(cp, op)()
-            return carry
-
-        lax.fori_loop(0, 4, one, 0)
-
-    def load_rows(l, f, slot, op):
-        zs = pl.ds(f * (nz // 4), nz // 4)
-
-        def one(i, carry):
-            j, g = i // 4, i % 4
-            cp = pltpu.make_async_copy(
-                G.at[l * PER + 8 + j, zs, :, :, :, cols(g)],
-                wbuf.at[slot, pl.ds(j * (nz // 4), nz // 4), :, :, g],
-                wsem.at[slot, i],
-            )
-            getattr(cp, op)()
-            return carry
-
-        lax.fori_loop(0, 16, one, 0)
+    def load_unit(u, slot):
+        pltpu.make_async_copy(G.at[u], wbuf.at[slot], wsem.at[slot]).start()
+
+    def load_rows(l, f, slot):
+        q = nz // 4
+        for j in range(4):
+            pltpu.make_async_copy(
+                G.at[l * PER + 8 + j, pl.ds(f * q, q)], wbuf.at[slot, pl.ds(j * q, q)], wsem.at[slot]
+            ).start()
+
+    def loaded(slot):
+        pltpu.make_async_copy(G.at[0], wbuf.at[slot], wsem.at[slot]).wait()
 
     def w_cols(slot, g):
-        return wbuf[slot, :, :, :, g].reshape(D, BLK)
+        return wbuf[slot, :, :, :, :, cols(g)].reshape(D, BLK)
 
     def w_rows(slot, i):
-        q = nz // 4
+        return wbuf[slot, pl.ds(i * (nz // 4), nz // 4)].reshape(BLK, D)
+
+    def stacked(chips):
+        return jnp.concatenate([w[:, g * BLK : (g + 1) * BLK] for w in chips for g in range(4)], axis=0)
+
+    def chip(slot, i):
+        return wbuf[slot, i // (n * n), (i // n) % n, i % n]
+
+    def o_rows(slot, i):
+        per = nb // 16
         return jnp.concatenate(
-            [wbuf[slot, pl.ds(i * q, q), :, :, g].reshape(BLK, BLK) for g in range(4)], axis=1
+            [stacked([chip(slot, j * quarter + i * per + w) for w in range(per)]) for j in range(4)], axis=1
         )
 
-    def o_rows(slot, i):
-        if nz == 4:
-            parts = [wbuf[slot, j, i // n, i % n].reshape(BLK, BLK) for j in range(4)]
-        else:
-            q = nz // 4
-            parts = [wbuf[slot, pl.ds(j * q, q)].reshape(D, BLK)[i * BLK : (i + 1) * BLK] for j in range(4)]
-        return jnp.concatenate(parts, axis=1)
+    def o_cols(slot, i):
+        return stacked([chip(slot, i * quarter + w) for w in range(quarter)])
 
     def norm_rows(z, gain, shift):
         average = jnp.mean(z, axis=1, keepdims=True)
@@ -560,8 +608,10 @@
     def do_outer(l, j, slot, part):
         cs = cols(j)
         rs = slice(part * half, (part + 1) * half)
-        w = wbuf[slot].reshape(FF, BLK)
-        xs[rs, cs] = mid[rs, cs] + dot(act[rs, :], w) + outer_bias[pl.ds(l, 1), cs]
+        y = mid[rs, cs] + outer_bias[pl.ds(l, 1), cs]
+        for i in range(4):
+            y = y + dot(act[rs, i * D : (i + 1) * D], o_cols(slot, i))
+        xs[rs, cs] = y
 
     def do_norm2(l):
         gain, shift = row(second_gain, l), row(second_shift, l)
@@ -571,7 +621,9 @@
             normed, r, y = norm_rows(xs[rs, :], gain, shift)
             n2[l, rs, :] = normed.astype(BF)
             r2[l, rs, :] = r
-            xb[rs, :] = y.astype(BF)
+            yb = y.astype(BF)
+            xb[rs, :] = yb
+            ctx[rs, :] = yb
             xs[rs, :] = jnp.where(l == LAYERS - 1, cot[rs, :].astype(F32), y)
             return carry
 
@@ -613,6 +665,13 @@
                 pl.when(l == 0)(lambda: save_prob("wait"))
                 do_norm2(l)
 
+    def load(s, slot):
+        l, k = 1 - s // PER, s % PER
+        rows = (k < 8) & (k % 2 == 0)
+        pl.when(rows)(lambda: load_rows(l, k // 2, slot))
+        unit = l * PER + jnp.where(k < 8, 4 + k // 2, jnp.where(k == 8, 3, k - 9))
+        pl.when(jnp.logical_not(rows))(lambda: load_unit(unit, slot))
+
     lag = (comm.stages - 1) * gap + 1
 
     def main(t, carry):
@@ -628,14 +687,20 @@
                 def _():
                     comm.sibling(1 - core, v).wait_recv()
 
-            load_unit(v, slot, "start")
+            load_unit(v, slot)
 
         comm.tick(t, 0)
         pl.when(t == 1)(init_x)
 
         @pl.when(ready)
         def _():
-            load_unit(v, slot, "wait")
+            loaded(slot)
+
+            @pl.when(v == UNITS - 1)
+            def _():
+                load(0, 0)
+                load(1, 1)
+
             compute(v, slot, 0)
 
         comm.tick(t, 1)
@@ -675,16 +740,9 @@
             device_id_type=MESH,
         ).wait_recv()
 
-    def load(s, slot, op):
-        l, k = 1 - s // PER, s % PER
-        rows = (k < 8) & (k % 2 == 0)
-        pl.when(rows)(lambda: load_rows(l, k // 2, slot, op))
-        unit = l * PER + jnp.where(k < 8, 4 + k // 2, jnp.where(k == 8, 3, k - 9))
-        pl.when(jnp.logical_not(rows))(lambda: load_unit(unit, slot, op))
-
     def next_weights(s):
-        load(s, s % 3, "wait")
-        pl.when(s + 2 < UNITS)(lambda: load(s + 2, (s + 2) % 3, "start"))
+        loaded(s % 3)
+        pl.when(s + 2 < UNITS)(lambda: load(s + 2, (s + 2) % 3))
         return s % 3
 
     def keep_sum(l, k, values):
@@ -712,10 +770,7 @@
         keep_sum(l, at_shift, colsum(sum_g))
         keep_sum(l, at_bias, colsum(sum_z))
 
-    results(xb, layer_output, 0, "start")
-    load(0, 0, "start")
-    load(1, 1, "start")
-    results(xb, layer_output, 0, "wait")
+    results(ctx, layer_output, 0, "start")
 
     def layer_back(i, carry):
         l = LAYERS - 1 - i
@@ -750,6 +805,8 @@
             bg[l, 0, 2 * i4 + 1 : 2 * i4 + 2, :] = sums[:, 128:]
             qkv[0, :, sl] = gc
             gcT[sl, :] = gc.T
+
+        pl.when(i == 0)(lambda: results(ctx, layer_output, 0, "wait"))
 
         @pl.when(i == 1)
         def _():
@@ -902,6 +959,8 @@
     )
     dma = pltpu.SemaphoreType.DMA
     scratch = [
+        pltpu.VMEM((2, D), BF),
+        *(pltpu.VMEM((LAYERS, w), F32) for w in (D, D, D, FF, D, D, D, D, D)),
         pltpu.VMEM((UNITS, R, D), BF),
         pltpu.VMEM((T, D), BF),
         pltpu.VMEM((T, D), BF),
@@ -920,30 +979,28 @@
         pltpu.VMEM((D, T), BF),
         pltpu.VMEM((D, T), BF),
         pltpu.VMEM((D, T), BF),
-        pltpu.VMEM((3, nz, n, n, 4, R, BLK), BF),
+        pltpu.VMEM((3, nz, n, n, R, D), BF),
         pltpu.VMEM((LAYERS, 10, 8, 128), F32),
         pltpu.VMEM((LAYERS, plane, 10, 8, 128), F32),
         pltpu.VMEM((LAYERS, 10, 8, 128), F32),
         pltpu.VMEM((LAYERS, nz, 10, 8, 128), F32),
         pltpu.VMEM((8, D), F32),
-        dma((slots, sems)),
+        dma((slots,)),
         dma((slots, sems)),
         dma((slots,)),
-        dma((UNITS,)),
-        dma((UNITS + 32,)),
-        dma((3, 16)),
+        dma((slots,)),
+        dma((2,)),
+        dma((3,)),
         dma((6,)),
         dma(()),
+        dma((10,)),
         dma((6,)),
-        dma((3, plane)),
-        dma((3, plane)),
-        dma((3, nz)),
-        dma((3, nz)),
+        dma((3, 4)),
     ]
     out = pl.pallas_call(
         functools.partial(kernel, nz, n, gap, slots),
         out_shape=out_shape,
-        in_specs=[smem, smem, hbm, hbm, vmem, hbm, hbm, hbm, hbm] + [vmem] * 9,
+        in_specs=[smem, smem] + [hbm] * 16,
         out_specs=(hbm, hbm, vmem, hbm, hbm),
         scratch_shapes=scratch,
         compiler_params=pltpu.CompilerParams(

time: 302 us -> 288 us (0.954)
  Pallas kernels: 300 us -> 286 us
    pallas_call x1, Pallas kernels: 296 us -> 282 us  [on_device(): pl.pallas_call(functools.partial(kernel, nz, n, gap, slots), out_shape=ou...]
where the time goes in v3:
time: 288 us; the launch traced here: 287 us
  Pallas kernels  286 us (99%)
    pallas_call x1, Pallas kernels, on_device(): pl.pallas_call(functools.partial(kernel, nz, n, gap, slots), out_shape=ou...  282 us

profile of v3, /device:TPU:0, one launch (start us, length us, event | category | flops | bytes accessed | tf_op | source)
XLA Modules:
  0.0 286.5 jit_solution(15740733487557006974)
XLA Ops:
  0.6 281.8 %shard_map.241 = (bf16[2,256,1024]{2,1,0:T(8,128)(2,1)}, bf16[2,256,1024]{2,1,0:T(8,128)(2,1)}, f32[2,10,8,128]{3,2,1,0:T(8,128)}, bf16[24,4,2,2,64,1024]{5,4,3,2,1,0:T(8,128)(2,1)}, bf16[16,512,512]{2,1,0:T(8,128)(2,1)}) custom-call(s32[2]{0:T(128)} %lengths.1, s32[2]{0:T(128)} %separators.1, bf16[2,256,1024]{2,1,0:T(8,128)(2,1)} %hidden.1, ...), custom_call_target="tpu_custom_call" | custom-call | flops 60000002048 | bytes 200000000 | tf_op jit(solution)/shard_map/pallas_call | solution.py:1000
  282.4 3.9 %shard_map.242 = (bf16[2,256,1024]{2,1,0:T(8,128)(2,1)}, bf16[2,256,1024]{2,1,0:T(8,128)(2,1)}, f32[2,1024]{1,0:T(2,128)}, f32[2,1024]{1,0:T(2,128)}, f32[2,1024...) custom-call(bf16[2,256,1024]{2,1,0:T(8,128)(2,1)} %get-tuple-element.12.first, ...), custom_call_target="tpu_custom_call" | custom-call | tf_op jit(solution)/shard_map/pallas_call | solution.py:1032

commit v4 on v3

--- a/solution.py
+++ b/solution.py
@@ -16,7 +16,7 @@
 PER = 12
 SPLIT = 640
 BLK = 256
-ROWS = 64
+ROWS = 256
 EPSILON = 1e-12
 MASKED = -1000000000.0
 MESH = pl.DeviceIdType.MESH
@@ -216,12 +216,12 @@
 
     def tick(self, t, part):
         order = [self.stages, *reversed(range(self.stages))]
-        cut = len(order) // 2
+        cuts = (0, len(order) // 3 + 1, 2 * len(order) // 3 + 1, len(order))
         for core in (0, 1):
 
             @pl.when(self.c == core)
             def _():
-                for k in order[:cut] if part == 0 else order[cut:]:
+                for k in order[cuts[part] : cuts[part + 1]]:
                     u = t - k * self.gap
                     for par in (0, 1):
 
@@ -577,10 +577,14 @@
 
         lax.fori_loop(lo, hi, pair, 0)
 
-    def do_out(l, slot):
+    def do_out(l, slot, part):
+        if part == 2:
+            return do_norm1(l)
         for g in range(4):
             sl = slice(g * BLK, (g + 1) * BLK)
             mid[:, sl] = xs[:, sl] + dot(ctx[...], w_cols(slot, g)) + output_bias[pl.ds(l, 1), sl]
+
+    def do_norm1(l):
         gain, shift = row(first_gain, l), row(first_shift, l)
 
         def rows_of(i, carry):
@@ -607,7 +611,7 @@
 
     def do_outer(l, j, slot, part):
         cs = cols(j)
-        rs = slice(part * half, (part + 1) * half)
+        rs = pl.ds(pl.multiple_of(part * half, half), half)
         y = mid[rs, cs] + outer_bias[pl.ds(l, 1), cs]
         for i in range(4):
             y = y + dot(act[rs, i * D : (i + 1) * D], o_cols(slot, i))
@@ -634,30 +638,33 @@
 
     def compute(v, slot, part):
         l, k = v // PER, v % PER
-        pl.when(k < 3)(lambda: do_qkv(l, k, slot, 2 * part, 2 * part + 2))
-
-        @pl.when((k >= 2) & (k <= 4))
-        def _():
-            if part == 0:
-                do_attention(l, jnp.where(k == 2, 0, jnp.where(k == 3, 1, 5)), jnp.where(k == 2, 0, jnp.where(k == 3, 3, 8)))
-            else:
-                do_attention(l, jnp.where(k == 2, 0, 3), jnp.where(k == 2, 1, jnp.where(k == 3, 5, 3)))
-
-        if part == 1:
-
-            @pl.when(k == 4)
+
+        def choose(*of_k):
+            out = jnp.int32(of_k[-1])
+            for i, value in enumerate(of_k[:-1]):
+                out = jnp.where(k == i, value, out)
+            return out
+
+        pl.when(k < 3)(lambda: do_qkv(l, k, slot, (0, 2, 3)[part], (2, 3, 4)[part]))
+
+        first = {0: (0, 0, 0, 1, 4, 7), 1: (0, 0, 0, 2, 5), 2: (0, 0, 0, 3, 6)}[part]
+        when = {0: (k >= 3) & (k <= 5), 1: (k == 3) | (k == 4), 2: (k >= 2) & (k <= 4)}[part]
+        pl.when(when)(lambda: do_attention(l, choose(*first), choose(*first) + 1))
+
+        if part:
+
+            @pl.when(k == 5)
             def _():
-                pl.when(l == 0)(lambda: save_prob("start"))
-                do_out(l, (v + 2) % 3)
-
-        @pl.when((k >= 5) & (k < 8))
-        def _():
-            if part == 0:
-                do_inner(l, jnp.where(k == 5, 0, 4 * (k - 4)), jnp.where(k == 5, 4, 4 * (k - 4) + 2))
-            else:
-                do_inner(l, jnp.where(k == 5, 4, 4 * (k - 4) + 2), 4 * (k - 4) + 4)
-
-        pl.when(k >= 8)(lambda: do_outer(l, k - 8, slot, part))
+                if part == 1:
+                    pl.when(l == 0)(lambda: save_prob("start"))
+                do_out(l, (v + 1) % 3, part)
+
+        lo = {0: (0, 0, 0, 0, 0, 0, 0, 7, 14), 1: (0, 0, 0, 0, 0, 0, 3, 10), 2: (0, 0, 0, 0, 0, 0, 5, 12)}[part]
+        hi = {0: (0, 0, 0, 0, 0, 0, 3, 10, 16), 1: (0, 0, 0, 0, 0, 0, 5, 12), 2: (0, 0, 0, 0, 0, 0, 7, 14)}[part]
+        pl.when((k >= 6) & (k <= (8 if part == 0 else 7)))(lambda: do_inner(l, choose(*lo), choose(*hi)))
+
+        when = {0: k > 8, 1: k >= 8, 2: k == 8}[part]
+        pl.when(when)(lambda: do_outer(l, k - 8, slot, jnp.where(k == 8, part - 1, part)))
         if part == 1:
 
             @pl.when(k == PER - 1)
@@ -679,16 +686,6 @@
         slot = (v + 3 * lag) % 3
         ready = (v >= 0) & (v < UNITS)
 
-        @pl.when(ready)
-        def _():
-            for core in (0, 1):
-
-                @pl.when(c == core)
-                def _():
-                    comm.sibling(1 - core, v).wait_recv()
-
-            load_unit(v, slot)
-
         comm.tick(t, 0)
         pl.when(t == 1)(init_x)
 
@@ -705,7 +702,19 @@
 
         comm.tick(t, 1)
         pl.when(ready)(lambda: compute(v, slot, 1))
-
+        comm.tick(t, 2)
+
+        @pl.when((v >= -1) & (v < UNITS - 1))
+        def _():
+            for core in (0, 1):
+
+                @pl.when(c == core)
+                def _():
+                    comm.sibling(1 - core, v + 1).wait_recv()
+
+            load_unit(v + 1, (slot + 1) % 3)
+
+        pl.when(ready)(lambda: compute(v, slot, 2))
         return carry
 
     lax.fori_loop(0, UNITS + comm.stages * gap, main, 0)
@@ -834,7 +843,7 @@
             ctx[:, cs] = dq.astype(BF)
             return carry
 
-        lax.fori_loop(0, HEADS // 2, pair, 0)
+        lax.fori_loop(0, HEADS // 2, pair, 0, unroll=2)
         keep_sum(l, 9, colsum(dqs8[...]))
 
         @pl.when(i == 0)

time: 288 us -> 276 us (0.958)
  Pallas kernels: 286 us -> 274 us
    pallas_call x1, Pallas kernels: 282 us -> 270 us  [on_device(): pl.pallas_call(functools.partial(kernel, nz, n, gap, slots), out_shape=ou...]
where the time goes in v4:
time: 276 us; the launch traced here: 275 us
  Pallas kernels  274 us (99%)
    pallas_call x1, Pallas kernels, on_device(): pl.pallas_call(functools.partial(kernel, nz, n, gap, slots), out_shape=ou...  270 us

profile of v4, /device:TPU:0, one launch (start us, length us, event | category | flops | bytes accessed | tf_op | source)
XLA Modules:
  0.0 275.2 jit_solution(2551165721225603389)
XLA Ops:
  0.6 270.5 %shard_map.241 = (bf16[2,256,1024]{2,1,0:T(8,128)(2,1)}, bf16[2,256,1024]{2,1,0:T(8,128)(2,1)}, f32[2,10,8,128]{3,2,1,0:T(8,128)}, bf16[24,4,2,2,64,1024]{5,4,3,2,1,0:T(8,128)(2,1)}, bf16[16,512,512]{2,1,0:T(8,128)(2,1)}) custom-call(s32[2]{0:T(128)} %lengths.1, s32[2]{0:T(128)} %separators.1, bf16[2,256,1024]{2,1,0:T(8,128)(2,1)} %hidden.1, ...), custom_call_target="tpu_custom_call" | custom-call | flops 60000002048 | bytes 200000000 | tf_op jit(solution)/shard_map/pallas_call | solution.py:1009
  271.1 3.9 %shard_map.242 = (bf16[2,256,1024]{2,1,0:T(8,128)(2,1)}, bf16[2,256,1024]{2,1,0:T(8,128)(2,1)}, f32[2,1024]{1,0:T(2,128)}, f32[2,1024]{1,0:T(2,128)}, f32[2,1024...) custom-call(bf16[2,256,1024]{2,1,0:T(8,128)(2,1)} %get-tuple-element.12.first, ...), custom_call_target="tpu_custom_call" | custom-call | tf_op jit(solution)/shard_map/pallas_call | solution.py:1041

commit v5 on v4

--- a/solution.py
+++ b/solution.py
@@ -34,10 +34,10 @@
 
 
 class Comm:
-    def __init__(self, nz, n, gathered, stg, ssem, rsem, sib_s, sib_r, slots, gap):
+    def __init__(self, nz, n, gathered, stg, ssem, rsem, sib_s, sib_r, slots, ticks):
         self.nz, self.n, self.G, self.stg = nz, n, gathered, stg
         self.ssem, self.rsem, self.sib_s, self.sib_r = ssem, rsem, sib_s, sib_r
-        self.slots, self.gap = slots, gap
+        self.slots, self.ticks = slots, ticks
         self.b = lax.axis_index("batch")
         self.c = lax.axis_index("blk")
         self.z, self.y, self.x = self.b // (n * n), (self.b // n) % n, self.b % n
@@ -222,7 +222,7 @@
             @pl.when(self.c == core)
             def _():
                 for k in order[cuts[part] : cuts[part + 1]]:
-                    u = t - k * self.gap
+                    u = t - self.ticks[k]
                     for par in (0, 1):
 
                         @pl.when((u >= 0) & (u < UNITS) & (u % 2 == par))
@@ -232,7 +232,7 @@
                             else:
                                 self.run(core, par, u, k, "start")
 
-    def barrier(self):
+    def barrier(self, meanwhile):
         bar = pltpu.get_barrier_semaphore()
         plane, me = 2 * self.n * self.n, self.place()
 
@@ -245,8 +245,9 @@
             pl.semaphore_signal(bar, inc=1, device_id=self.along((self.z + i) % self.nz), device_id_type=MESH)
             return carry
 
-        lax.fori_loop(1, plane, in_plane, 0)
-        lax.fori_loop(1, self.nz, along_z, 0)
+        lax.fori_loop(1, plane, in_plane, 0, unroll=plane <= 8)
+        lax.fori_loop(1, self.nz, along_z, 0, unroll=plane <= 8)
+        meanwhile()
         pl.semaphore_wait(bar, plane - 1 + self.nz - 1)
 
     def place(self):
@@ -260,8 +261,8 @@
 
 
 class Total:
-    def __init__(self, comm, phase, l, lo, hi, bg, planes, part, lines, total, sems):
-        self.comm, self.phase, self.l, self.rows = comm, phase, l, pl.ds(lo, hi - lo)
+    def __init__(self, comm, phase, lo, hi, bg, planes, part, lines, total, sems):
+        self.comm, self.phase, self.rows = comm, phase, pl.ds(lo, hi - lo)
         self.bg, self.planes, self.part, self.lines, self.total = bg, planes, part, lines, total
         self.sems = sems
 
@@ -281,32 +282,32 @@
         )
 
     def send(self, second):
-        comm, l, rows = self.comm, self.l, self.rows
+        comm, rows = self.comm, self.rows
         src, dst, me, count = self.ends(second)
 
         def one(i, carry):
             peer = (me + i) % count
             to = comm.along(peer) if second else comm.at(peer)
-            self.copy(second, src.at[l, rows], dst.at[l, me, rows], to).start()
+            self.copy(second, src.at[rows], dst.at[me, rows], to).start()
             return carry
 
-        lax.fori_loop(1, count, one, 0)
+        lax.fori_loop(1, count, one, 0, unroll=count <= 8)
 
     def every(self, second):
         _, dst, _, count = self.ends(second)
-        all_of = dst.at[self.l, pl.ds(0, count - 1), self.rows]
+        all_of = dst.at[pl.ds(0, count - 1), self.rows]
         return self.copy(second, all_of, all_of, (self.comm.b, 1 - self.comm.c))
 
     def add(self, second):
         src, buf, me, count = self.ends(second)
         out = self.total if second else self.part
         self.every(second).wait_recv()
-        buf[self.l, me, self.rows] = src[self.l, self.rows]
+        buf[me, self.rows] = src[self.rows]
 
         def one(i, acc):
-            return acc + buf[self.l, i, self.rows]
-
-        out[self.l, self.rows] = lax.fori_loop(1, count, one, buf[self.l, 0, self.rows])
+            return acc + buf[i, self.rows]
+
+        out[self.rows] = lax.fori_loop(1, count, one, buf[0, self.rows], unroll=count <= 8)
         self.every(second).wait_send()
 
     def start(self):
@@ -336,7 +337,7 @@
 def kernel(
     nz,
     n,
-    gap,
+    ticks,
     slots,
     lengths,
     separators,
@@ -412,7 +413,7 @@
     T = xs.shape[0]
     half = T // 2
     quarter = nb // 4
-    comm = Comm(nz, n, G, stg, ssem, rsem, sib_s, sib_r, slots, gap)
+    comm = Comm(nz, n, G, stg, ssem, rsem, sib_s, sib_r, slots, ticks)
     c = comm.c
     other = (comm.b, 1 - c)
     ctx = xin
@@ -474,9 +475,11 @@
         for i, (src, dst) in enumerate(vectors):
             getattr(pltpu.make_async_copy(src, dst, vsem.at[i]), op)()
 
-    stage_in()
-    small("start")
-    comm.barrier()
+    def begin():
+        stage_in()
+        small("start")
+
+    comm.barrier(begin)
     exchange("start")
     place()
 
@@ -679,7 +682,7 @@
         unit = l * PER + jnp.where(k < 8, 4 + k // 2, jnp.where(k == 8, 3, k - 9))
         pl.when(jnp.logical_not(rows))(lambda: load_unit(unit, slot))
 
-    lag = (comm.stages - 1) * gap + 1
+    lag = ticks[comm.stages - 1] + 1
 
     def main(t, carry):
         v = t - lag
@@ -717,7 +720,7 @@
         pl.when(ready)(lambda: compute(v, slot, 2))
         return carry
 
-    lax.fori_loop(0, UNITS + comm.stages * gap, main, 0)
+    lax.fori_loop(0, UNITS + ticks[comm.stages], main, 0)
 
     def results(src, out, base, op):
         mine = pl.ds(pl.multiple_of(c * half, half), half)
@@ -756,7 +759,7 @@
 
     def keep_sum(l, k, values):
         for i in range(values.shape[1] // 128):
-            bg[l, k, i : i + 1, :] = values[:, i * 128 : (i + 1) * 128]
+            bg[(1 - l) * 10 + k, i : i + 1, :] = values[:, i * 128 : (i + 1) * 128]
 
     def norm_back(l, source, normed, r_ref, gain_ref, at_shift, at_bias, keep):
         gain = row(gain_ref, l)
@@ -784,8 +787,7 @@
     def layer_back(i, carry):
         l = LAYERS - 1 - i
         s0 = i * PER
-        norm_back(l, xs, n2, r2, second_gain, 8, 6, mid)
-        pl.when(i == 1)(totals[0].start)
+        norm_back(l, xs, n2, r2, second_gain, 7, 5, mid)
 
         def ff(f, carry):
             slot = next_weights(s0 + 2 * f)
@@ -793,8 +795,8 @@
                 cs = cols(f * 4 + i4)
                 gh = dot(xb[...], o_rows(slot, i4), 1, 1) * gp[l, :, cs].astype(F32)
                 sums = colsum(fold(gh))
-                bg[l, 2 + f, 2 * i4 : 2 * i4 + 1, :] = sums[:, :128]
-                bg[l, 2 + f, 2 * i4 + 1 : 2 * i4 + 2, :] = sums[:, 128:]
+                bg[(1 - l) * 10 + 1 + f, 2 * i4 : 2 * i4 + 1, :] = sums[:, :128]
+                bg[(1 - l) * 10 + 1 + f, 2 * i4 + 1 : 2 * i4 + 2, :] = sums[:, 128:]
                 act[:, cs] = gh.astype(BF)
             slot = next_weights(s0 + 2 * f + 1)
             for i4 in range(4):
@@ -803,15 +805,15 @@
             return carry
 
         lax.fori_loop(0, 4, ff, 0)
-        pl.when(i == 1)(totals[0].middle)
-        norm_back(l, mid, n1, r1, first_gain, 7, 1, mid)
+        norm_back(l, mid, n1, r1, first_gain, 6, 0, mid)
+        pl.when(i == 1)(totals[0].start)
         slot = next_weights(s0 + 8)
         for i4 in range(4):
             sl = slice(i4 * BLK, (i4 + 1) * BLK)
             gc = dot(xb[...], w_rows(slot, i4), 1, 1).astype(BF)
             sums = colsum(fold(gc.astype(F32)))
-            bg[l, 0, 2 * i4 : 2 * i4 + 1, :] = sums[:, :128]
-            bg[l, 0, 2 * i4 + 1 : 2 * i4 + 2, :] = sums[:, 128:]
+            bg[(1 - l) * 10 + 8, 2 * i4 : 2 * i4 + 1, :] = sums[:, :128]
+            bg[(1 - l) * 10 + 8, 2 * i4 + 1 : 2 * i4 + 2, :] = sums[:, 128:]
             qkv[0, :, sl] = gc
             gcT[sl, :] = gc.T
 
@@ -820,8 +822,6 @@
         @pl.when(i == 1)
         def _():
             load_prob("wait")
-            totals[0].finish()
-            totals[1].start()
 
         def pair(hp, carry):
             cs = cols(hp, 2 * HEAD)
@@ -843,7 +843,12 @@
             ctx[:, cs] = dq.astype(BF)
             return carry
 
-        lax.fori_loop(0, HEADS // 2, pair, 0, unroll=2)
+        def four(j, carry):
+            lax.fori_loop(0, 4, lambda h, x: pair(4 * j + h, x), 0, unroll=2)
+            pl.when((i == 1) & (j == 0))(totals[0].middle)
+            return carry
+
+        lax.fori_loop(0, HEADS // 8, four, 0)
         keep_sum(l, 9, colsum(dqs8[...]))
 
         @pl.when(i == 0)
@@ -852,8 +857,7 @@
 
         @pl.when(i == 1)
         def _():
-            totals[2].start()
-            totals[1].middle()
+            totals[1].start()
 
 
         slot = next_weights(s0 + 9)
@@ -864,7 +868,12 @@
         for i4 in range(4):
             sl = slice(i4 * BLK, (i4 + 1) * BLK)
             mid[:, sl] += dot(dkT[...], w_rows(slot, i4), 0, 1)
-        pl.when(i == 1)(totals[2].middle)
+
+        @pl.when(i == 1)
+        def _():
+            totals[1].middle()
+            totals[0].finish()
+
         slot = next_weights(s0 + 11)
         for i4 in range(4):
             sl = slice(i4 * BLK, (i4 + 1) * BLK)
@@ -877,53 +886,48 @@
         getattr(pltpu.make_async_copy(P0, prob, psem), op)()
 
     totals = [
-        Total(comm, phase, l, lo, hi, bg, planes, part, lines, total, asems)
-        for phase, (l, lo, hi) in enumerate(((1, 0, 10), (0, 0, 9), (0, 9, 10)))
+        Total(comm, phase, lo, hi, bg, planes, part, lines, total, asems)
+        for phase, (lo, hi) in enumerate(((0, 18), (18, 20)))
     ]
     lax.fori_loop(0, LAYERS, layer_back, 0)
     results(xb, input_gradient, 3, "start")
     totals[1].finish()
-    totals[2].finish()
     results(xb, input_gradient, 3, "wait")
     arrived(xb, layer_output, 0)
     arrived(xb, input_gradient, 3)
 
 
 def finish(first, second, total, *rest):
-    outs, (buf, into, outof) = rest[:9], rest[9:]
+    outs, (buf, rows, *sums), (into, outof) = rest[:9], rest[9:18], rest[18:]
     half = first.shape[1] // 2
     moves = []
     for i, (src, dst) in enumerate(((first, outs[0]), (second, outs[1]))):
         for j in range(2):
-            rows = pl.ds(j * half, half)
+            part = pl.ds(j * half, half)
             k = 2 * i + j
             moves.append(
                 (
-                    pltpu.make_async_copy(src.at[:, rows], buf.at[k], into.at[k]),
-                    pltpu.make_async_copy(buf.at[k], dst.at[:, rows], outof.at[k]),
+                    pltpu.make_async_copy(src.at[:, part], buf.at[k], into.at[k]),
+                    pltpu.make_async_copy(buf.at[k], dst.at[:, part], outof.at[k]),
                 )
             )
+    small = pltpu.make_async_copy(total, rows, into.at[4])
+    small.start()
     for here, _ in moves:
         here.start()
-    for l in range(LAYERS):
-        for k, out, at in (
-            (9, outs[2], 0),
-            (0, outs[3], 0),
-            (1, outs[4], 0),
-            (2, outs[5], 0),
-            (3, outs[5], 1),
-            (4, outs[5], 2),
-            (5, outs[5], 3),
-            (6, outs[6], 0),
-            (7, outs[7], 0),
-            (8, outs[8], 0),
-        ):
-            for i in range(8):
-                out[l : l + 1, at * D + i * 128 : at * D + (i + 1) * 128] = total[l, k, i : i + 1, :]
+    small.wait()
+    done = [there for _, there in moves]
+    for m, ks in enumerate(((9,), (8,), (0,), (1, 2, 3, 4), (5,), (6,), (7,))):
+        for l in range(LAYERS):
+            for at, k in enumerate(ks):
+                for i in range(8):
+                    sums[m][l : l + 1, at * D + i * 128 : at * D + (i + 1) * 128] = rows[(1 - l) * 10 + k, i : i + 1, :]
+        done.append(pltpu.make_async_copy(sums[m], outs[2 + m], outof.at[4 + m]))
+        done[-1].start()
     for here, there in moves:
         here.wait()
         there.start()
-    for _, there in moves:
+    for there in done:
         there.wait()
 
 
@@ -951,7 +955,10 @@
     nz, n = sizes(nb)
     gap = 2 if nb <= 16 else 1
     stages = 1 + (n - 1) + (nz - 1) + (n - 1)
-    slots = (stages + 1) * gap
+    ticks = [k * gap for k in range(stages + 1)]
+    if gap == 2:
+        ticks[-2:] = ticks[-2] - 1, ticks[-1] - 1
+    slots = ticks[-1] + gap
     plane = 2 * n * n
     T = 2 * hidden.shape[1]
     R = D // nb
@@ -962,7 +969,7 @@
     out_shape = (
         jax.ShapeDtypeStruct(hidden.shape, BF),
         jax.ShapeDtypeStruct(hidden.shape, BF),
-        jax.ShapeDtypeStruct((LAYERS, 10, 8, 128), F32),
+        jax.ShapeDtypeStruct((LAYERS * 10, 8, 128), F32),
         jax.ShapeDtypeStruct((UNITS, nz, n, n, R, D), BF),
         jax.ShapeDtypeStruct((HEADS, T, T), BF),
     )
@@ -989,10 +996,10 @@
         pltpu.VMEM((D, T), BF),
         pltpu.VMEM((D, T), BF),
         pltpu.VMEM((3, nz, n, n, R, D), BF),
-        pltpu.VMEM((LAYERS, 10, 8, 128), F32),
-        pltpu.VMEM((LAYERS, plane, 10, 8, 128), F32),
-        pltpu.VMEM((LAYERS, 10, 8, 128), F32),
-        pltpu.VMEM((LAYERS, nz, 10, 8, 128), F32),
+        pltpu.VMEM((LAYERS * 10, 8, 128), F32),
+        pltpu.VMEM((plane, LAYERS * 10, 8, 128), F32),
+        pltpu.VMEM((LAYERS * 10, 8, 128), F32),
+        pltpu.VMEM((nz, LAYERS * 10, 8, 128), F32),
         pltpu.VMEM((8, D), F32),
         dma((slots,)),
         dma((slots, sems)),
@@ -1004,10 +1011,10 @@
         dma(()),
         dma((10,)),
         dma((6,)),
-        dma((3, 4)),
+        dma((2, 4)),
     ]
     out = pl.pallas_call(
-        functools.partial(kernel, nz, n, gap, slots),
+        functools.partial(kernel, nz, n, ticks, slots),
         out_shape=out_shape,
         in_specs=[smem, smem] + [hbm] * 16,
         out_specs=(hbm, hbm, vmem, hbm, hbm),
@@ -1037,19 +1044,24 @@
         second_shift,
     )
     half = hidden.shape[1] // 2
+    sums = [query_bias, value_bias, output_bias, inner_bias, outer_bias, first_shift, second_shift]
     return tuple(
         pl.pallas_call(
             finish,
             out_shape=(
                 jax.ShapeDtypeStruct(hidden.shape, BF),
                 jax.ShapeDtypeStruct(hidden.shape, BF),
-                *(jax.ShapeDtypeStruct(b.shape, F32) for b in (
-                    query_bias, value_bias, output_bias, inner_bias, outer_bias, first_shift, second_shift
-                )),
+                *(jax.ShapeDtypeStruct(b.shape, F32) for b in sums),
             ),
-            in_specs=[hbm, hbm, vmem],
-            out_specs=(hbm, hbm) + (vmem,) * 7,
-            scratch_shapes=[pltpu.VMEM((4, 2, half, D), BF), dma((4,)), dma((4,))],
+            in_specs=[hbm] * 3,
+            out_specs=(hbm,) * 9,
+            scratch_shapes=[
+                pltpu.VMEM((4, 2, half, D), BF),
+                pltpu.VMEM((LAYERS * 10, 8, 128), F32),
+                *(pltpu.VMEM(b.shape, F32) for b in sums),
+                dma((5,)),
+                dma((11,)),
+            ],
         )(out[0], out[1], out[2])
     )
 

time: 276 us -> 271 us (0.982)
  Pallas kernels: 274 us -> 269 us
    pallas_call x1, Pallas kernels: 270 us -> 266 us  [on_device(): pl.pallas_call(functools.partial(kernel, nz, n, ticks, slots), out_shape=...]
where the time goes in v5:
time: 271 us; the launch traced here: 270 us
  Pallas kernels  269 us (99%)
    pallas_call x1, Pallas kernels, on_device(): pl.pallas_call(functools.partial(kernel, nz, n, ticks, slots), out_shape=...  266 us

profile of v5, /device:TPU:0, one launch (start us, length us, event | category | flops | bytes accessed | tf_op | source)
XLA Modules:
  0.0 269.8 jit_solution(8719899844353316131)
XLA Ops:
  0.6 266.4 %shard_map.241 = (bf16[2,256,1024]{2,1,0:T(8,128)(2,1)}, bf16[2,256,1024]{2,1,0:T(8,128)(2,1)}, f32[20,8,128]{2,1,0:T(8,128)}, bf16[24,4,2,2,64,1024]{5,4,3,2,1,0:T(8,128)(2,1)}, bf16[16,512,512]{2,1,0:T(8,128)(2,1)}) custom-call(s32[2]{0:T(128)} %lengths.1, s32[2]{0:T(128)} %separators.1, bf16[2,256,1024]{2,1,0:T(8,128)(2,1)} %hidden.1, ...), custom_call_target="tpu_custom_call" | custom-call | flops 60000002048 | bytes 200000000 | tf_op jit(solution)/shard_map/pallas_call | solution.py:1016
  267.1 2.6 shard_map.242

commit v6 on v5

--- a/solution.py
+++ b/solution.py
@@ -16,7 +16,7 @@
 PER = 12
 SPLIT = 640
 BLK = 256
-ROWS = 256
+ROWS = 512
 EPSILON = 1e-12
 MASKED = -1000000000.0
 MESH = pl.DeviceIdType.MESH
@@ -218,14 +218,15 @@
         order = [self.stages, *reversed(range(self.stages))]
         cuts = (0, len(order) // 3 + 1, 2 * len(order) // 3 + 1, len(order))
         for core in (0, 1):
-
-            @pl.when(self.c == core)
-            def _():
-                for k in order[cuts[part] : cuts[part + 1]]:
-                    u = t - self.ticks[k]
-                    for par in (0, 1):
-
-                        @pl.when((u >= 0) & (u < UNITS) & (u % 2 == par))
+            for odd in (0, 1):
+
+                @pl.when((self.c == core) & (t % 2 == odd))
+                def _():
+                    for k in order[cuts[part] : cuts[part + 1]]:
+                        u = t - self.ticks[k]
+                        par = (odd + self.ticks[k]) % 2
+
+                        @pl.when((u >= 0) & (u < UNITS))
                         def _():
                             if k == self.stages:
                                 self.drain(core, par, u)
@@ -601,24 +602,21 @@
 
         lax.fori_loop(0, T // ROWS, rows_of, 0)
 
-    def do_inner(l, lo, hi):
-        def block(i, carry):
+    def do_inner(l, pair):
+        for of in (0, 1):
+            i = 2 * pair + of
             cs = cols(i)
-            h = dot(xb[...], w_cols((l * PER + 4 + i // 4) % 3, i % 4)) + inner_bias[pl.ds(l, 1), cs]
+            h = dot(xb[...], w_cols((l * PER + 4 + pair // 2) % 3, i % 4)) + inner_bias[pl.ds(l, 1), cs]
             cdf = 0.5 + 0.5 * lax.erf(h * (0.5**0.5))
             act[:, cs] = (h * cdf).astype(BF)
             gp[l, :, cs] = (cdf + h * (jnp.exp(-0.5 * h * h) * 0.3989422804014327)).astype(BF)
-            return carry
-
-        lax.fori_loop(lo, hi, block, 0)
-
-    def do_outer(l, j, slot, part):
+
+    def do_outer(l, j, slot):
         cs = cols(j)
-        rs = pl.ds(pl.multiple_of(part * half, half), half)
-        y = mid[rs, cs] + outer_bias[pl.ds(l, 1), cs]
+        y = mid[:, cs] + outer_bias[pl.ds(l, 1), cs]
         for i in range(4):
-            y = y + dot(act[rs, i * D : (i + 1) * D], o_cols(slot, i))
-        xs[rs, cs] = y
+            y = y + dot(act[:, i * D : (i + 1) * D], o_cols(slot, i))
+        xs[:, cs] = y
 
     def do_norm2(l):
         gain, shift = row(second_gain, l), row(second_shift, l)
@@ -662,12 +660,10 @@
                     pl.when(l == 0)(lambda: save_prob("start"))
                 do_out(l, (v + 1) % 3, part)
 
-        lo = {0: (0, 0, 0, 0, 0, 0, 0, 7, 14), 1: (0, 0, 0, 0, 0, 0, 3, 10), 2: (0, 0, 0, 0, 0, 0, 5, 12)}[part]
-        hi = {0: (0, 0, 0, 0, 0, 0, 3, 10, 16), 1: (0, 0, 0, 0, 0, 0, 5, 12), 2: (0, 0, 0, 0, 0, 0, 7, 14)}[part]
-        pl.when((k >= 6) & (k <= (8 if part == 0 else 7)))(lambda: do_inner(l, choose(*lo), choose(*hi)))
-
-        when = {0: k > 8, 1: k >= 8, 2: k == 8}[part]
-        pl.when(when)(lambda: do_outer(l, k - 8, slot, jnp.where(k == 8, part - 1, part)))
+        last = 7 if part == 2 else 8
+        pl.when((k >= 6) & (k <= last))(lambda: do_inner(l, 3 * (k - 6) + part))
+        if part != 1:
+            pl.when(k > 8 if part == 0 else k == 8)(lambda: do_outer(l, k - 8, slot))
         if part == 1:
 
             @pl.when(k == PER - 1)
@@ -844,7 +840,7 @@
             return carry
 
         def four(j, carry):
-            lax.fori_loop(0, 4, lambda h, x: pair(4 * j + h, x), 0, unroll=2)
+            lax.fori_loop(0, 4, lambda h, x: pair(4 * j + h, x), 0, unroll=4)
             pl.when((i == 1) & (j == 0))(totals[0].middle)
             return carry
 

time: 271 us -> 268 us (0.989)
  no operation moved by 1% of the time
where the time goes in v6:
time: 268 us; the launch traced here: 267 us
  Pallas kernels  267 us (100%)
    pallas_call x1, Pallas kernels, on_device(): pl.pallas_call(functools.partial(kernel, nz, n, ticks, slots), out_shape=...  264 us

profile of v6, /device:TPU:0, one launch (start us, length us, event | category | flops | bytes accessed | tf_op | source)
XLA Modules:
  0.0 267.4 jit_solution(12151154950097774064)
XLA Ops:
  0.6 264.0 %shard_map.241 = (bf16[2,256,1024]{2,1,0:T(8,128)(2,1)}, bf16[2,256,1024]{2,1,0:T(8,128)(2,1)}, f32[20,8,128]{2,1,0:T(8,128)}, bf16[24,4,2,2,64,1024]{5,4,3,2,1,0:T(8,128)(2,1)}, bf16[16,512,512]{2,1,0:T(8,128)(2,1)}) custom-call(s32[2]{0:T(128)} %lengths.1, s32[2]{0:T(128)} %separators.1, bf16[2,256,1024]{2,1,0:T(8,128)(2,1)} %hidden.1, ...), custom_call_target="tpu_custom_call" | custom-call | flops 60000002048 | bytes 200000000 | tf_op jit(solution)/shard_map/pallas_call | solution.py:1012
  264.7 2.6 shard_map.242

commit v7 on v6

--- a/solution.py
+++ b/solution.py
@@ -216,7 +216,7 @@
 
     def tick(self, t, part):
         order = [self.stages, *reversed(range(self.stages))]
-        cuts = (0, len(order) // 3 + 1, 2 * len(order) // 3 + 1, len(order))
+        cuts = (0, 4, 6, 7) if len(order) == 7 else (0, len(order) // 3 + 1, 2 * len(order) // 3 + 1, len(order))
         for core in (0, 1):
             for odd in (0, 1):
 
@@ -953,7 +953,7 @@
     stages = 1 + (n - 1) + (nz - 1) + (n - 1)
     ticks = [k * gap for k in range(stages + 1)]
     if gap == 2:
-        ticks[-2:] = ticks[-2] - 1, ticks[-1] - 1
+        ticks = [0, 2, 4, 6, 7, 9, 11]
     slots = ticks[-1] + gap
     plane = 2 * n * n
     T = 2 * hidden.shape[1]

time: 268 us -> 267 us (level)
  no operation moved by 1% of the time
where the time goes in v7:
time: 267 us; the launch traced here: 266 us
  Pallas kernels  266 us (100%)
    pallas_call x1, Pallas kernels, on_device(): pl.pallas_call(functools.partial(kernel, nz, n, ticks, slots), out_shape=...  263 us

profile of v7, /device:TPU:0, one launch (start us, length us, event | category | flops | bytes accessed | tf_op | source)
XLA Modules:
  0.0 266.5 jit_solution(9300082792072598024)
XLA Ops:
  0.6 263.1 %shard_map.241 = (bf16[2,256,1024]{2,1,0:T(8,128)(2,1)}, bf16[2,256,1024]{2,1,0:T(8,128)(2,1)}, f32[20,8,128]{2,1,0:T(8,128)}, bf16[24,4,2,2,64,1024]{5,4,3,2,1,0:T(8,128)(2,1)}, bf16[16,512,512]{2,1,0:T(8,128)(2,1)}) custom-call(s32[2]{0:T(128)} %lengths.1, s32[2]{0:T(128)} %separators.1, bf16[2,256,1024]{2,1,0:T(8,128)(2,1)} %hidden.1, ...), custom_call_target="tpu_custom_call" | custom-call | flops 60000002048 | bytes 200000000 | tf_op jit(solution)/shard_map/pallas_call | solution.py:1012
  263.8 2.6 shard_map.242
